TPU v7x, 512 devices: a whole 4x8x8 slice. The times are simulated.
512 devices in a mesh: dp: 32 (over z, x_lo, core), expert: 16 (over y, x_hi).
Axes of the slice: x: 4 (x_hi: 2, x_lo: 2; x = x_hi * 2 + x_lo), y: 8, z: 8, core: 2. Of those that a mesh axis runs over, the one named last changes fastest.
Arguments:
- grad_parts: bfloat16 [16, 32, 5120, 128], P('expert', 'dp'), may hold values from -3 to 3
- master: float32 [16, 5120, 128], P('expert', 'dp'), may hold values from -0.3125 to 0.3125
- moment: float32 [16, 5120, 128], P('expert', 'dp'), may hold values from -3 to 3
- second: float32 [16, 5120, 128], P('expert', 'dp'), may hold values from 0.0001 to 0.01
- down_weight: bfloat16 [16, 5120, 64], P('expert', 'dp'), may hold values from -0.75 to 0.75
- tokens: bfloat16 [65536, 5120], P(('dp', 'expert')), may hold values from -6 to 6
- routes: int32 [65536, 1], P(('dp', 'expert')), may hold values from 0 to 15; in each aligned block of 128 rows (0 to 127, 128 to 255, ...) at most 16 rows name the same one
- probs: float32 [65536], P(('dp', 'expert')), may hold values from 0.3 to 1
Outputs:
- new_master: float32 [16, 5120, 128], P('expert', 'dp')
- new_moment: float32 [16, 5120, 128], P('expert', 'dp')
- mixed: bfloat16 [65536, 5120], P(('dp', 'expert'))
Inputs may be any that keep to these rules, and one draw needn't show every extreme that they name: `routes`: among the 128 tokens of one device no expert is named more than 16 times; some expert is named exactly 16 times.
All inputs are finite; a program needn't handle non-finite values.
Results may differ from a plain program's by a relative error of at most 0.029.
Values may be sent and summed in bfloat16 or wider, within the bound.
No kernel may reach another device: no remote copies, remote signals or barrier semaphores. Data moves between devices by JAX's collectives and lax.ppermute only.
A program may use at most 64 MiB of HBM per device.

v0:
```python
import jax
import jax.numpy as jnp
from jax import lax
from jax.sharding import PartitionSpec as P

beta_one = 0.9
beta_two = 0.95
learn_rate = 0.005
decay_rate = 0.1
adam_eps = 1e-08
bias_one = 1.0 - 0.9**50
bias_two = 1.0 - 0.95**50


def adamw(weight, moment, second, grad):
    moment_new = beta_one * moment + (1.0 - beta_one) * grad
    second_new = beta_two * second + (1.0 - beta_two) * grad * grad
    update = moment_new / bias_one / (jnp.sqrt(second_new / bias_two) + adam_eps)
    return (weight - learn_rate * (update + decay_rate * weight), moment_new)


def shards(grad_parts, master, moment, second, down_weight, tokens, routes, probs):
    experts = lax.axis_size("expert")
    tok_rows = tokens.shape[0]
    cap_rows = 2 * tok_rows // experts
    width = tokens.shape[1]
    units = master.shape[2] // 2
    chosen = routes[:, 0]
    onehot = (chosen[:, None] == jnp.arange(experts, dtype=jnp.int32)[None, :]).astype(jnp.int32)
    before = jnp.cumsum(onehot, axis=0) - onehot
    position = jnp.sum(before * onehot, axis=1)
    target = chosen * cap_rows + position
    select = (jnp.arange(experts * cap_rows, dtype=jnp.int32)[:, None] == target[None, :]).astype(
        jnp.bfloat16
    )
    packed = jnp.dot(select, tokens, preferred_element_type=jnp.float32).astype(jnp.bfloat16)
    packed = packed.reshape(experts, cap_rows, width)
    total = lax.psum_scatter(
        grad_parts[0, 0].astype(jnp.float32).astype(jnp.bfloat16),
        "dp",
        scatter_dimension=0,
        tiled=True,
    ).astype(jnp.float32)
    new_weight, new_first = adamw(master[0], moment[0], second[0], total)
    short = new_weight.astype(jnp.bfloat16)
    gate_up, down = (
        lax.all_gather(short, "dp", axis=0, tiled=True),
        lax.all_gather(down_weight[0], "dp", axis=0, tiled=True),
    )
    arrived = lax.all_to_all(packed, "expert", split_axis=0, concat_axis=0, tiled=True)
    shape = arrived.shape
    flat = arrived.reshape(-1, width)
    both = jnp.dot(flat, gate_up, preferred_element_type=jnp.float32)
    hidden = (jax.nn.silu(both[:, :units]) * both[:, units:]).astype(jnp.bfloat16)
    result = lax.dot_general(
        hidden, down, (((1,), (1,)), ((), ())), preferred_element_type=jnp.float32
    )
    returned = lax.all_to_all(
        result.astype(jnp.bfloat16).reshape(shape),
        "expert",
        split_axis=0,
        concat_axis=0,
        tiled=True,
    )
    flat = returned.reshape(experts * cap_rows, width)
    gathered = lax.dot_general(
        select, flat, (((0,), (0,)), ((), ())), preferred_element_type=jnp.float32
    )
    mixed = (probs[:, None] * gathered).astype(jnp.bfloat16)
    return (new_weight[None], new_first[None], mixed)


def solution(mesh):
    in_specs = (
        P("expert", "dp", None, None),
        P("expert", "dp", None),
        P("expert", "dp", None),
        P("expert", "dp", None),
        P("expert", "dp", None),
        P(("dp", "expert"), None),
        P(("dp", "expert"), None),
        P(("dp", "expert")),
    )
    out_specs = (P("expert", "dp", None), P("expert", "dp", None), P(("dp", "expert"), None))
    return jax.shard_map(shards, mesh=mesh, in_specs=in_specs, out_specs=out_specs, check_vma=False)
```

profile of v0, /device:TPU:1, one launch (start us, length us, event | category | flops | bytes accessed | tf_op | source)
XLA Modules:
  0.0 300.6 jit_solution(1984467069334019880)
XLA Ops:
  7.2 0.0 copy-start
  7.2 0.0 reduce-scatter.2.cloned.1.call-start
  7.2 0.7 reduce-scatter.2.cloned.1.call-update
  7.9 0.7 fusion.13
  8.7 0.2 reduce_window_sum.11
  8.8 0.8 select_reduce_fusion
  9.7 0.7 multiply_add_fusion
  10.3 2.3 convolution_convert_fusion.1
  12.7 10.4 %all-to-all-start = ((bf16[16,16,5120]{2,1,0:T(8,128)(2,1)}), bf16[16,16,5120]{2,1,0:T(8,128)(2,1)}, u32[]{:S(2)}, u32[]{:S(2)}) async-start(bf16[16,16,5120]{2,1,0:T(8,128)(2,1)} %bitcast.37), calls=%async_computation.1 | async-start | bytes 5242880 | tf_op jit(solution)/shard_map/all_to_all | solution.py:50
  23.1 0.0 all-gather.3.cloned.1.call-start
  23.1 115.1 %reduce-scatter.2.cloned.1.call-done = bf16[160,128]{1,0:T(8,128)(2,1)} async-done(((bf16[5120,128]{1,0:T(8,128)(2,1)}), bf16[160,128]{1,0:T(8,128)(2,1)}) %reduce-scatter.2.cloned.1.call-update) | async-done | bytes 40976 | tf_op jit(solution)/shard_map/reduce_scatter | solution.py:38
  138.3 0.0 copy-done.1
  138.3 1.5 fusion.17
  139.8 0.0 all-gather.3.cloned.1.call-update
  139.8 0.1 copy.12
  140.0 47.8 %all-gather = bf16[1,5120,64]{2,0,1:T(2,128)(2,1)} all-gather(bf16[1,160,64]{2,0,1:T(2,128)(2,1)S(1)} %copy.12), channel_id=2, replica_groups=mesh['dp'=32,'expert'=16] {'dp'}, dimensions={1}, use_global_device_ids=true | all-gather | bytes 675840 | tf_op jit(solution)/shard_map/all_gather | solution.py:48
  187.8 4.8 %copy.13 = bf16[1,5120,64]{1,2,0:T(8,128)(2,1)S(1)} copy(bf16[1,5120,64]{2,0,1:T(2,128)(2,1)} %all-gather) | data formatting | bytes 1310720 | tf_op jit(solution)/shard_map/all_gather | solution.py:48
  192.5 0.0 all-to-all-done
  192.5 24.7 %all-gather.3.cloned.1.call-done = bf16[5120,128]{1,0:T(8,128)(2,1)} async-done(((bf16[160,128]{1,0:T(8,128)(2,1)}), bf16[5120,128]{1,0:T(8,128)(2,1)}) %all-gather.3.cloned.1.call-update) | async-done | bytes 1310736 | tf_op jit(solution)/shard_map/all_gather | solution.py:47
  217.2 3.1 %fusion.18 = f32[256,128]{0,1:T(8,128)S(1)} fusion(bf16[256,5120]{1,0:T(8,128)(2,1)} %bitcast.8, bf16[5120,128]{1,0:T(8,128)(2,1)} %all-gather.3.cloned.1.call-done), kind=kOutput, calls=%fused_computation.29 | convolution fusion | flops 335544320 | bytes 4063232 | tf_op jit(solution)/shard_map/dot_general | solution.py:53
  220.3 0.9 convolution_convert_fusion
  221.2 0.0 copy-start.5
  221.2 70.9 %all_to_all.10 = bf16[16,16,5120]{2,1,0:T(8,128)(2,1)S(1)} all-to-all(bf16[16,16,5120]{2,1,0:T(8,128)(2,1)S(1)} %bitcast.38), channel_id=1, replica_groups=mesh['dp'=32,'expert'=16] {'expert'}, dimensions={0} | all-to-all | bytes 5242880 | tf_op jit(solution)/shard_map/all_to_all | solution.py:58
  292.1 1.6 fusion
  (9 shorter events, 0.0 us)
Async XLA Ops:
  7.2 3.2 %copy-start = (bf16[128,5120]{1,0:T(8,128)(2,1)S(1)}, bf16[128,5120]{1,0:T(8,128)(2,1)}, u32[]{:S(2)}) copy-start(bf16[128,5120]{1,0:T(8,128)(2,1)} %param.13) | copy-start | bytes 3932164
  7.2 131.1 %reduce-scatter.2.cloned.1.call-start = ((), (), s32[]{:S(2)}) async-start(), calls=%async_computation.3 | async-start | bytes 1351680 | tf_op jit(solution)/shard_map/reduce_scatter | solution.py:38
  12.7 125.6 %copy-start.1 = (f32[1,160,128]{2,1,0:T(8,128)S(1)}, f32[1,160,128]{2,1,0:T(8,128)}, u32[]{:S(2)}) copy-start(f32[1,160,128]{2,1,0:T(8,128)} %param.11) | copy-start | bytes 245764
  12.7 125.6 %copy-start.2 = (f32[1,160,128]{2,1,0:T(8,128)S(1)}, f32[1,160,128]{2,1,0:T(8,128)}, u32[]{:S(2)}) copy-start(f32[1,160,128]{2,1,0:T(8,128)} %param.10) | copy-start | bytes 245764
  12.7 125.6 %copy-start.3 = (f32[1,160,128]{2,1,0:T(8,128)S(1)}, f32[1,160,128]{2,1,0:T(8,128)}, u32[]{:S(2)}) copy-start(f32[1,160,128]{2,1,0:T(8,128)} %param.9) | copy-start | bytes 245764
  12.7 127.1 %copy-start.4 = (bf16[1,160,64]{1,2,0:T(8,128)(2,1)S(1)}, bf16[1,160,64]{1,2,0:T(8,128)(2,1)}, u32[]{:S(2)}) copy-start(bf16[1,160,64]{1,2,0:T(8,128)(2,1)} %param.12) | copy-start | bytes 61444
  12.7 179.8 %all-to-all-start = ((bf16[16,16,5120]{2,1,0:T(8,128)(2,1)}), bf16[16,16,5120]{2,1,0:T(8,128)(2,1)}, u32[]{:S(2)}, u32[]{:S(2)}) async-start(bf16[16,16,5120]{2,1,0:T(8,128)(2,1)} %bitcast.37), calls=%async_computation.1 | async-start | bytes 5242880 | tf_op jit(solution)/shard_map/all_to_all | solution.py:50
  23.1 194.1 %all-gather.3.cloned.1.call-start = ((), (), s32[]{:S(2)}) async-start(), calls=%async_computation.4 | async-start | bytes 1351680 | tf_op jit(solution)/shard_map/all_gather | solution.py:47
  221.2 70.9 %copy-start.5 = (f32[128]{0:T(128)S(1)}, f32[128]{0:T(128)}, u32[]{:S(2)}) copy-start(f32[128]{0:T(128)} %param.15) | copy-start | bytes 1540
Sparse Core Ops, SparseCore 0:
  10.8 127.4 reduce-scatter.1
  141.2 75.9 all-gather.2
where the time goes:
time: 301 us
  waiting for transfers between devices  140 us (47%)
  blocking collectives  119 us (40%)
  between operations  14.1 us (5%)
  starting transfers between devices  10.5 us (3%)
  matrix products  7.95 us (3%)
  local copies, waits for them, and re-layouts  4.91 us (2%)
  other arithmetic  3.94 us (1%)
    reduce_scatter x1, waiting for transfers between devices, shards(): lax.psum_scatter(grad_parts[0, 0].astype(jnp.float32).astype(jnp.bfloat16...  115 us
    all_to_all x1, blocking collectives, shards(): lax.all_to_all(result.astype(jnp.bfloat16).reshape(shape), 'expert', spli...  70.9 us
    all_gather x1, blocking collectives, shards(): lax.all_gather(down_weight[0], 'dp', axis=0, tiled=True)  47.8 us
    all_gather x1, waiting for transfers between devices, shards(): lax.all_gather(short, 'dp', axis=0, tiled=True)  24.7 us
    all_to_all x1, starting transfers between devices, shards(): lax.all_to_all(packed, 'expert', split_axis=0, concat_axis=0, tiled=True)  10.4 us
  transfers between devices with their start and end apart: 3, of which 2 were waited for; matrix products, arithmetic and copies ran while one was open for 4% of the time, Pallas kernels for 0%

commit v1 on v0

v1 whole, which is shorter than its diff:
```python
import functools

import jax
import jax.numpy as jnp
from jax import lax
from jax.experimental import pallas as pl
from jax.experimental.pallas import tpu as pltpu
from jax.sharding import Mesh, PartitionSpec as P

beta_one = 0.9
beta_two = 0.95
learn_rate = 0.005
decay_rate = 0.1
adam_eps = 1e-08
bias_one = 1.0 - 0.9**50
bias_two = 1.0 - 0.95**50

Z, XL, C, Y, XH = 8, 2, 2, 8, 2
GROUP = Z * XL
EXPERTS = Y * XH
D = 5120
ROWS = 160
COLS = 320
TOK = 128
UNITS = 64
SWAP = ((0, 1), (1, 0))
LIMIT = 56 * 1024 * 1024

f32 = jnp.float32
bf16 = jnp.bfloat16


def params(**kw):
    return pltpu.CompilerParams(vmem_limit_bytes=LIMIT, **kw)


def cost(flops, nbytes):
    return pl.CostEstimate(flops=flops, bytes_accessed=nbytes, transcendentals=0)


def pack_kernel(x_ref, o_ref):
    x = x_ref[...]
    half = TOK // 2
    for k in range(2):
        part = x[:, k * COLS : (k + 1) * COLS]
        o_ref[k] = jnp.concatenate([part[:half], part[half:]], axis=1)


def pack(tokens):
    return pl.pallas_call(
        pack_kernel,
        out_shape=jax.ShapeDtypeStruct((GROUP, TOK // 2, 2 * COLS), bf16),
        grid=(Z,),
        in_specs=[pl.BlockSpec((TOK, 2 * COLS), lambda i: (0, i))],
        out_specs=pl.BlockSpec((2, TOK // 2, 2 * COLS), lambda i: (i, 0, 0)),
        compiler_params=params(),
        cost_estimate=cost(0, 2 * TOK * D * 2),
    )(tokens)


def add_kernel(c_ref, g_ref, r_ref, route_ref, o_ref):
    total = g_ref[:, 0].astype(f32) + r_ref[...].astype(f32)
    o_ref[:, :ROWS] = total.astype(bf16)
    rows = jnp.broadcast_to(route_ref[...].astype(f32), (16, TOK)).astype(bf16)
    for i in range(o_ref.shape[0]):
        o_ref[i, ROWS:] = rows


def add(core, grads, received, route_row):
    n = 8
    return pl.pallas_call(
        add_kernel,
        out_shape=jax.ShapeDtypeStruct((GROUP, ROWS + 16, TOK), bf16),
        grid_spec=pltpu.PrefetchScalarGridSpec(
            num_scalar_prefetch=1,
            grid=(GROUP // n,),
            in_specs=[
                pl.BlockSpec((n, 1, ROWS, 128), lambda i, c: (i, c[0], 0, 0)),
                pl.BlockSpec((n, ROWS, 128), lambda i, c: (i, 0, 0)),
                pl.BlockSpec((1, TOK), lambda i, c: (0, 0)),
            ],
            out_specs=pl.BlockSpec((n, ROWS + 16, TOK), lambda i, c: (i, 0, 0)),
        ),
        compiler_params=params(),
        cost_estimate=cost(0, 3 * GROUP * ROWS * 256),
    )(core, grads, received, route_row)


def adam_kernel(g_ref, w_ref, m_ref, s_ref, nw_ref, nm_ref, short_ref, route_ref):
    total = g_ref[0, :ROWS].astype(f32)
    for i in range(1, GROUP):
        total = total + g_ref[i, :ROWS].astype(f32)
    weight = w_ref[...]
    moment_new = beta_one * m_ref[...] + (1.0 - beta_one) * total
    second_new = beta_two * s_ref[...] + (1.0 - beta_two) * total * total
    update = moment_new / bias_one / (jnp.sqrt(second_new / bias_two) + adam_eps)
    new_weight = weight - learn_rate * (update + decay_rate * weight)
    nw_ref[...] = new_weight
    nm_ref[...] = moment_new
    short_ref[...] = new_weight.astype(bf16)
    for i in range(GROUP):
        route_ref[i : i + 1, :] = g_ref[i, ROWS : ROWS + 16].astype(f32)[0:1]


def adam(arrived, master, moment, second):
    return pl.pallas_call(
        adam_kernel,
        out_shape=(
            jax.ShapeDtypeStruct((ROWS, 128), f32),
            jax.ShapeDtypeStruct((ROWS, 128), f32),
            jax.ShapeDtypeStruct((ROWS, 128), bf16),
            jax.ShapeDtypeStruct((GROUP, TOK), f32),
        ),
        compiler_params=params(),
        cost_estimate=cost(0, GROUP * ROWS * 256 + 5 * ROWS * 512),
    )(arrived, master, moment, second)


def partial_kernel(ids_ref, own_ref, other_ref, x_ref, route_ref, o_ref, w_scr, x_scr, r_scr, acc_scr):
    core = ids_ref[0]
    high = ids_ref[1]
    half = TOK // 2
    mine = pl.multiple_of(core * ROWS, 32)
    theirs = pl.multiple_of((1 - core) * ROWS, 32)
    for e in range(EXPERTS):
        w_scr[pl.ds(mine, ROWS), e * 128 : (e + 1) * 128] = own_ref[e]
        w_scr[pl.ds(theirs, ROWS), e * 128 : (e + 1) * 128] = other_ref[e]
    columns = jnp.transpose(route_ref[...])
    for s in range(GROUP):
        x_scr[s * TOK : s * TOK + half, :] = x_ref[s, :, :COLS]
        x_scr[s * TOK + half : (s + 1) * TOK, :] = x_ref[s, :, COLS:]
        r_scr[s * TOK : (s + 1) * TOK, :] = jnp.broadcast_to(columns[:, s : s + 1], (TOK, 128))
    step = 512
    for e in range(0, EXPERTS, 2):
        first = (e + high).astype(f32)
        second = (e + 1 - high).astype(f32)

        def rows(i, carry):
            at = pl.ds(pl.multiple_of(i * step, step), step)
            both = jnp.dot(
                x_scr[at, :], w_scr[:, e * 128 : (e + 2) * 128], preferred_element_type=f32
            )
            route = r_scr[at, :]
            kept = acc_scr[at, :] if e else jnp.zeros((step, 128), f32)
            kept = jnp.where(route == first, both[:, :128], kept)
            kept = jnp.where(route == second, both[:, 128:], kept)
            if e + 2 < EXPERTS:
                acc_scr[at, :] = kept
            else:
                o_ref[at, :] = kept.astype(bf16)
            return carry

        lax.fori_loop(0, GROUP * TOK // step, rows, 0)


def partial_sums(ids, own, other, x, route):
    return pl.pallas_call(
        partial_kernel,
        out_shape=jax.ShapeDtypeStruct((GROUP * TOK, 128), bf16),
        in_specs=[pl.BlockSpec(memory_space=pltpu.SMEM)]
        + [pl.BlockSpec(memory_space=pltpu.VMEM)] * 4,
        out_specs=pl.BlockSpec(memory_space=pltpu.VMEM),
        scratch_shapes=[
            pltpu.VMEM((COLS, EXPERTS * 128), bf16),
            pltpu.VMEM((GROUP * TOK, COLS), bf16),
            pltpu.VMEM((GROUP * TOK, 128), f32),
            pltpu.VMEM((GROUP * TOK, 128), f32),
        ],
        compiler_params=params(),
        cost_estimate=cost(2 * GROUP * TOK * COLS * EXPERTS * 128, 4 * 1024 * 1024),
    )(ids, own, other, x, route)


def hidden_kernel(p_ref, route_ref, o_ref):
    total = p_ref[0].astype(f32)
    for i in range(1, GROUP):
        total = total + p_ref[i].astype(f32)
    gate = total[:, :UNITS]
    up = total[:, UNITS:]
    hidden = gate * jax.nn.sigmoid(gate) * up
    route = jnp.broadcast_to(route_ref[...].astype(f32), (TOK, UNITS))
    o_ref[...] = jnp.concatenate([hidden, route], axis=1).astype(bf16)


def hidden_units(parts, route_column):
    return pl.pallas_call(
        hidden_kernel,
        out_shape=jax.ShapeDtypeStruct((TOK, 128), bf16),
        compiler_params=params(),
        cost_estimate=cost(0, GROUP * TOK * 256),
    )(parts, route_column)


def down_kernel(own_ref, other_ref, d_ref, o_own_ref, o_other_ref, h_scr):
    @pl.when(pl.program_id(0) == 0)
    def _():
        lane = lax.broadcasted_iota(jnp.int32, (2 * TOK, 128), 1)
        both = jnp.concatenate([own_ref[...], other_ref[...]], axis=0).astype(f32)
        hidden = jnp.concatenate([both[:, :UNITS], both[:, :UNITS]], axis=1)
        route = jnp.concatenate([both[:, UNITS:], both[:, UNITS:]], axis=1)
        for y in range(Y):
            expert = jnp.where(lane < UNITS, 2.0 * y, 2.0 * y + 1.0)
            h_scr[:, y * 128 : (y + 1) * 128] = jnp.where(route == expert, hidden, 0.0).astype(bf16)

    total = jnp.zeros((2 * TOK, COLS), f32)
    for y in range(0, Y, 2):
        weights = jnp.concatenate([d_ref[0, y], d_ref[0, y + 1]], axis=1)
        total = total + lax.dot_general(
            h_scr[:, y * 128 : (y + 2) * 128],
            weights,
            (((1,), (1,)), ((), ())),
            preferred_element_type=f32,
        )
    o_own_ref[0] = total[:TOK].astype(bf16)
    o_other_ref[0] = total[TOK:].astype(bf16)


def down_project(own, other, down):
    return pl.pallas_call(
        down_kernel,
        out_shape=(
            jax.ShapeDtypeStruct((Z, TOK, COLS), bf16),
            jax.ShapeDtypeStruct((Z, TOK, COLS), bf16),
        ),
        grid=(Z,),
        in_specs=[
            pl.BlockSpec((TOK, 128), lambda i: (0, 0)),
            pl.BlockSpec((TOK, 128), lambda i: (0, 0)),
            pl.BlockSpec((1, Y, COLS, 128), lambda i: (i, 0, 0, 0)),
        ],
        out_specs=(
            pl.BlockSpec((1, TOK, COLS), lambda i: (i, 0, 0)),
            pl.BlockSpec((1, TOK, COLS), lambda i: (i, 0, 0)),
        ),
        scratch_shapes=[pltpu.VMEM((2 * TOK, EXPERTS * UNITS), bf16)],
        compiler_params=params(),
        cost_estimate=cost(2 * 2 * TOK * 1024 * 2560, 8 * 1024 * 1024),
    )(own, other, down)


def mix_kernel(c_ref, own_ref, other_ref, p_ref, o_ref):
    first_core = c_ref[0] == 0
    own = own_ref[0].astype(f32)
    other = other_ref[0].astype(f32)
    even = jnp.where(first_core, own, other)
    odd = jnp.where(first_core, other, own)
    whole = jnp.concatenate(
        [even[:, :ROWS], odd[:, :ROWS], even[:, ROWS:], odd[:, ROWS:]], axis=1
    )
    o_ref[...] = (p_ref[...] * whole).astype(bf16)


def mix(core, own, other, probs):
    return pl.pallas_call(
        mix_kernel,
        out_shape=jax.ShapeDtypeStruct((TOK, D), bf16),
        grid=(Z,),
        in_specs=[
            pl.BlockSpec(memory_space=pltpu.SMEM),
            pl.BlockSpec((1, TOK, COLS), lambda i: (i, 0, 0)),
            pl.BlockSpec((1, TOK, COLS), lambda i: (i, 0, 0)),
            pl.BlockSpec((TOK, 1), lambda i: (0, 0)),
        ],
        out_specs=pl.BlockSpec((TOK, 2 * COLS), lambda i: (0, i)),
        compiler_params=params(),
        cost_estimate=cost(0, 4 * TOK * D),
    )(core, own, other, probs)


def shards(grad_parts, master, moment, second, down_weight, tokens, routes, probs):
    core = lax.axis_index("c")
    low = lax.axis_index("xl")
    high = lax.axis_index("xh")
    core_id = core.reshape(1).astype(jnp.int32)
    group = ("z", "xl")

    grads = grad_parts.reshape(GROUP, C, ROWS, 128)
    sent = lax.dynamic_index_in_dim(grads, 1 - core, axis=1, keepdims=False)
    received = lax.ppermute(sent, "c", SWAP)

    down = down_weight[0]
    beside = lax.ppermute(down, "xh", SWAP)
    pair = jnp.where(
        high == 0, jnp.concatenate([down, beside], 1), jnp.concatenate([beside, down], 1)
    )
    beside = lax.ppermute(pair, "xl", SWAP)
    pair = jnp.where(low == 0, jnp.concatenate([pair, beside], 0), jnp.concatenate([beside, pair], 0))
    down_all = lax.all_gather(pair, ("z", "y"), axis=0, tiled=False).reshape(Z, Y, COLS, 128)

    packed = pack(tokens)
    chunk = add(core_id, grads, received, routes.reshape(1, TOK))
    arrived = lax.all_to_all(chunk, group, 0, 0, tiled=True)
    packed, arrived = lax.optimization_barrier((packed, arrived))
    columns = lax.all_to_all(packed, group, 0, 0, tiled=True)

    new_master, new_moment, short, route_all = adam(arrived, master[0], moment[0], second[0])
    pair_short = jnp.concatenate([short, lax.ppermute(short, "xh", SWAP)], axis=0)
    own = lax.all_gather(pair_short, "y", axis=0, tiled=True).reshape(EXPERTS, ROWS, 128)
    other = lax.ppermute(own, "c", SWAP)

    ids = jnp.stack([core, high]).astype(jnp.int32)
    parts = partial_sums(ids, own, other, columns, route_all)
    parts = lax.all_to_all(parts.reshape(GROUP, TOK, 128), group, 0, 0, tiled=True)
    hidden = hidden_units(parts, routes)
    beside = lax.ppermute(hidden, "c", SWAP)
    out_own, out_other = down_project(hidden, beside, down_all)
    out_other = lax.ppermute(out_other, "c", SWAP)
    mixed = mix(core_id, out_own, out_other, probs.reshape(TOK, 1))
    return new_master[None], new_moment[None], mixed


def solution(mesh):
    fine = Mesh(mesh.devices.reshape(Z, XL, C, Y, XH), ("z", "xl", "c", "y", "xh"))
    dp, expert = ("z", "xl", "c"), ("y", "xh")
    both = dp + expert
    in_specs = (
        P(expert, dp, None, None),
        P(expert, dp, None),
        P(expert, dp, None),
        P(expert, dp, None),
        P(expert, dp, None),
        P(both, None),
        P(both, None),
        P(both),
    )
    out_specs = (P(expert, dp, None), P(expert, dp, None), P(both, None))
    return jax.shard_map(shards, mesh=fine, in_specs=in_specs, out_specs=out_specs, check_vma=False)
```

time: 301 us -> 189 us (0.63)
  waiting for transfers between devices: 140 us -> 40.8 us
  blocking collectives: 119 us -> 24.9 us
  starting transfers between devices: 10.5 us -> 57.6 us
  Pallas kernels: 0 us -> 38.3 us
  matrix products: 7.95 us -> 0 us
  local copies, waits for them, and re-layouts: 4.91 us -> 9.68 us
    reduce_scatter x1 -> x0, waiting for transfers between devices: 115 us -> none  [shards(): lax.psum_scatter(grad_parts[0, 0].astype(jnp.float32).astype(jnp.bfloat16...]
    all_to_all x1 -> x0, blocking collectives: 70.9 us -> none  [shards(): lax.all_to_all(result.astype(jnp.bfloat16).reshape(shape), 'expert', spli...]
    ppermute x0 -> x7, starting transfers between devices: none -> 38.8 us  [the longest x1 10.5 us: shards(): received = lax.ppermute(sent, 'c', SWAP)]
    pallas_call x0 -> x7, Pallas kernels: none -> 38.3 us  [the longest x1 13 us: partial_sums(): pl.pallas_call(partial_kernel, out_shape=jax.ShapeDtypeStruct((GROUP * TO...]
    all_to_all x1 -> x3, waiting for transfers between devices: 0.01 us -> 30.8 us  [the longest x1 15.5 us: shards(): arrived = lax.all_to_all(chunk, group, 0, 0, tiled=True)]
    all_gather x1, waiting for transfers between devices: 24.7 us -> 0.01 us  [shards(): lax.all_gather(pair, ('z', 'y'), axis=0, tiled=False)]
    all_gather x1, blocking collectives: 47.8 us -> 24.9 us  [shards(): lax.all_gather(pair_short, 'y', axis=0, tiled=True)]
    ppermute x0 -> x7, waiting for transfers between devices: none -> 9.98 us  [the longest x1 2.4 us: shards(): lax.ppermute(short, 'xh', SWAP)]
  transfers between devices with their start and end apart: 3 -> 11, of which waited for: 2 -> 9; matrix products, arithmetic and copies ran while one was open for 4% -> 2% of each run, Pallas kernels for 0% -> 13%
where the time goes in v1:
time: 189 us; the launch traced here: 188 us
  starting transfers between devices  57.6 us (30%)
  waiting for transfers between devices  40.8 us (22%)
  Pallas kernels  38.3 us (20%)
  blocking collectives  24.9 us (13%)
  between operations  14.2 us (8%)
  local copies, waits for them, and re-layouts  9.68 us (5%)
  other arithmetic  2.15 us (1%)
    all_gather x1, blocking collectives, shards(): lax.all_gather(pair_short, 'y', axis=0, tiled=True)  24.9 us
    all_to_all x1, waiting for transfers between devices, shards(): arrived = lax.all_to_all(chunk, group, 0, 0, tiled=True)  15.5 us
    all_to_all x1, waiting for transfers between devices, shards(): lax.all_to_all(parts.reshape(GROUP, TOK, 128), group, 0, 0, tiled=True)  15.3 us
    pallas_call x1, Pallas kernels, partial_sums(): pl.pallas_call(partial_kernel, out_shape=jax.ShapeDtypeStruct((GROUP * TO...  13 us
    ppermute x1, starting transfers between devices, shards(): received = lax.ppermute(sent, 'c', SWAP)  10.5 us
    ppermute x1, starting transfers between devices, shards(): other = lax.ppermute(own, 'c', SWAP)  8.45 us
    pallas_call x1, Pallas kernels, down_project(): pl.pallas_call(down_kernel, out_shape=(jax.ShapeDtypeStruct((Z, TOK, COLS...  7.89 us
    all_to_all x1, starting transfers between devices, shards(): lax.all_to_all(parts.reshape(GROUP, TOK, 128), group, 0, 0, tiled=True)  7.86 us
  transfers between devices with their start and end apart: 11, of which 9 were waited for; matrix products, arithmetic and copies ran while one was open for 2% of the time, Pallas kernels for 13%

profile of v1, /device:TPU:1, one launch (start us, length us, event | category | flops | bytes accessed | tf_op | source)
XLA Modules:
  0.0 187.6 jit_solution(18092109406887273340)
XLA Ops:
  8.1 5.5 %collective-permute-start.4 = (bf16[160,64]{1,0:T(8,128)(2,1)S(1)}, bf16[160,64]{1,0:T(8,128)(2,1)S(1)}, u32[]{:S(2)}, u32[]{:S(2)}) collective-permute-start(bf16[160,64]{1,0:T(8,128)(2,1)S(1)} %bitcast.25), channel_id=1, source_target_pairs={{0,1},{1,0},{2,3},{3,2},{4,5},{5,4},{6,7},{7,6},{8,9},{9,8},{10,11... | collective-permute-start | bytes 61448 | tf_op jit(solution)/shard_map/ppermute | solution.py:282
  15.0 3.3 %collective-permute-start.5 = (bf16[160,128]{1,0:T(8,128)(2,1)S(1)}, bf16[160,128]{1,0:T(8,128)(2,1)S(1)}, u32[]{:S(2)}, u32[]{:S(2)}) collective-permute-start(bf16[160,128]{1,0:T(8,128)(2,1)S(1)} %maximum_select_fusion.1), channel_id=1, source_target_pairs={{0,32},{32,0},{1,33},{33,1},{2,34},{34,2},{3,35},{35,3},{4,36},{36... | collective-permute-start | bytes 122888 | tf_op jit(solution)/shard_map/ppermute | solution.py:286
  18.4 1.4 collective-permute-done.5
  21.6 10.5 %collective-permute-start = (bf16[16,160,128]{2,1,0:T(8,128)(2,1)S(1)}, bf16[16,160,128]{2,1,0:T(8,128)(2,1)S(1)}, u32[]{:S(2)}, u32[]{:S(2)}) collective-permute-start(bf16[16,160,128]{2,1,0:T(8,128)(2,1)S(1)} %dynamic-slice_bitcast_fusion), channel_id=1, source_target_pairs={{0,16},{16,0},{1,17},{17,1},{2,18},{18,2},{3,19},{19,3},{4,20},{20... | collective-permute-start | bytes 1966088 | tf_op jit(solution)/shard_map/ppermute | solution.py:279
  32.1 1.7 collective-permute-done.r_ref
  34.6 2.1 %shard_map.104 = bf16[16,176,128]{2,1,0:T(8,128)(2,1)} custom-call(s32[1]{0:T(128)} %bitcast.c_ref, bf16[16,2,160,128]{3,2,1,0:T(8,128)(2,1)} %bitcast.20, bf16[16,160,128]{2,1,0:T(8,128)(2,1)} %copy-done.4, s32[1,128]{1,0:T(1,128)} %bitcast.31), custom_call_target="tpu_custom_call" | custom-call | bytes 1966080 | tf_op jit(solution)/shard_map/pallas_call | solution.py:71
  36.7 5.7 %all-to-all-start = ((bf16[16,176,128]{2,1,0:T(8,128)(2,1)}), bf16[16,176,128]{2,1,0:T(8,128)(2,1)S(1)}, u32[]{:S(2)}, u32[]{:S(2)}) async-start(bf16[16,176,128]{2,1,0:T(8,128)(2,1)} %shard_map.104), calls=%async_computation | async-start | bytes 1441792 | tf_op jit(solution)/shard_map/all_to_all | solution.py:292
  42.4 5.6 %shard_map.103 = bf16[16,64,640]{2,1,0:T(8,128)(2,1)} custom-call(bf16[128,5120]{1,0:T(8,128)(2,1)} %x_ref.1), custom_call_target="tpu_custom_call" | custom-call | bytes 2621440 | tf_op jit(solution)/shard_map/pallas_call | solution.py:50
  48.1 15.5 %all-to-all-done.g_ref = bf16[16,176,128]{2,1,0:T(8,128)(2,1)S(1)} async-done(((bf16[16,176,128]{2,1,0:T(8,128)(2,1)}), bf16[16,176,128]{2,1,0:T(8,128)(2,1)S(1)}, u32[]{:S(2)}, u32[]{:S(2)}) %all-to-all-start) | async-done | bytes 720928 | tf_op jit(solution)/shard_map/all_to_all | solution.py:292
  63.6 5.2 %all-to-all-start.1 = ((bf16[16,64,640]{2,1,0:T(8,128)(2,1)}), bf16[16,64,640]{2,1,0:T(8,128)(2,1)S(1)}, u32[]{:S(2)}, u32[]{:S(2)}) async-start(bf16[16,64,640]{2,1,0:T(8,128)(2,1)} %shard_map.103), calls=%async_computation.1 | async-start | bytes 2621440 | tf_op jit(solution)/shard_map/all_to_all | solution.py:294
  68.8 2.0 %shard_map.105 = (f32[160,128]{1,0:T(8,128)}, f32[160,128]{1,0:T(8,128)}, bf16[160,128]{1,0:T(8,128)(2,1)}, f32[16,128]{1,0:T(8,128)}) custom-call(bf16[16,176,128]{2,1,0:T(8,128)(2,1)} %copy-done, f32[160,128]{1,0:T(8,128)} %bitcast.27, f32[160,128]{1,0:T(8,128)} %bitcast.28, f32[160,128]{1,0:T(8,128)} %bitcast.29), custom_call_target="tpu_custom_call" | custom-call | bytes 1064960 | tf_op jit(solution)/shard_map/pallas_call | solution.py:106
  70.8 4.3 %collective-permute-start.1 = (bf16[160,128]{1,0:T(8,128)(2,1)}, bf16[160,128]{1,0:T(8,128)(2,1)S(1)}, u32[]{:S(2)}, u32[]{:S(2)}) collective-permute-start(bf16[160,128]{1,0:T(8,128)(2,1)} %get-tuple-element.14), channel_id=1, source_target_pairs={{0,1},{1,0},{2,3},{3,2},{4,5},{5,4},{6,7},{7,6},{8,9},{9,8},{10,11... | collective-permute-start | bytes 122888 | tf_op jit(solution)/shard_map/ppermute | solution.py:297
  75.2 2.4 %collective-permute-done.1 = bf16[160,128]{1,0:T(8,128)(2,1)S(1)} collective-permute-done((bf16[160,128]{1,0:T(8,128)(2,1)}, bf16[160,128]{1,0:T(8,128)(2,1)S(1)}, u32[]{:S(2)}, u32[]{:S(2)}) %collective-permute-start.1) | collective-permute-done | bytes 40992 | tf_op jit(solution)/shard_map/ppermute | solution.py:297
  78.3 24.9 %all_gather.7 = bf16[2560,128]{1,0:T(8,128)(2,1)S(1)} all-gather(bf16[320,128]{1,0:T(8,128)(2,1)S(1)} %pad_maximum_fusion), channel_id=1, replica_groups=mesh['z'=8,'xl'=2,'c'=2,'y'=8,'xh'=2] {'y'}, dimensions={0}, use_global_device_ids=true | all-gather | bytes 737280 | tf_op jit(solution)/shard_map/all_gather | solution.py:298
  103.2 8.4 %collective-permute-start.2 = (bf16[16,160,128]{2,1,0:T(8,128)(2,1)S(1)}, bf16[16,160,128]{2,1,0:T(8,128)(2,1)S(1)}, u32[]{:S(2)}, u32[]{:S(2)}) collective-permute-start(bf16[16,160,128]{2,1,0:T(8,128)(2,1)S(1)} %bitcast.21), channel_id=1, source_target_pairs={{0,16},{16,0},{1,17},{17,1},{2,18},{18,2},{3,19},{19,3},{4,20},{20... | collective-permute-start | bytes 1966088 | tf_op jit(solution)/shard_map/ppermute | solution.py:299
  114.7 13.0 %shard_map.106 = bf16[2048,128]{1,0:T(8,128)(2,1)} custom-call(s32[2]{0:T(128)} %pad_add_fusion.ids_ref, bf16[16,160,128]{2,1,0:T(8,128)(2,1)} %bitcast.22, bf16[16,160,128]{2,1,0:T(8,128)(2,1)} %copy-done.8, bf16[16,64,640]{2,1,0:T(8,128)(2,1)} %copy-done.2, f32[16,128]{1,0:T(8,128)} %get-tuple-element.16.route_ref), custom_call_target="tpu_custom_call" | custom-call | flops 2684354560 | bytes 4194304 | tf_op jit(solution)/shard_map/pallas_call | solution.py:157
  127.6 7.9 %all-to-all-start.2 = ((bf16[16,128,128]{2,1,0:T(8,128)(2,1)}), bf16[16,128,128]{2,1,0:T(8,128)(2,1)S(1)}, u32[]{:S(2)}, u32[]{:S(2)}) async-start(bf16[16,128,128]{2,1,0:T(8,128)(2,1)} %bitcast.23), calls=%async_computation.2 | async-start | bytes 1048576 | tf_op jit(solution)/shard_map/all_to_all | solution.py:303
  136.3 15.3 %all-to-all-done.2.p_ref = bf16[16,128,128]{2,1,0:T(8,128)(2,1)S(1)} async-done(((bf16[16,128,128]{2,1,0:T(8,128)(2,1)}), bf16[16,128,128]{2,1,0:T(8,128)(2,1)S(1)}, u32[]{:S(2)}, u32[]{:S(2)}) %all-to-all-start.2) | async-done | bytes 524320 | tf_op jit(solution)/shard_map/all_to_all | solution.py:303
  152.3 1.8 shard_map.107.own_ref
  154.1 4.4 %collective-permute-start.3 = (bf16[128,128]{1,0:T(8,128)(2,1)}, bf16[128,128]{1,0:T(8,128)(2,1)S(1)}, u32[]{:S(2)}, u32[]{:S(2)}) collective-permute-start(bf16[128,128]{1,0:T(8,128)(2,1)} %shard_map.107.own_ref), channel_id=1, source_target_pairs={{0,16},{16,0},{1,17},{17,1},{2,18},{18,2},{3,19},{19,3},{4,20},{20... | collective-permute-start | bytes 98312 | tf_op jit(solution)/shard_map/ppermute | solution.py:305
  160.2 7.9 %shard_map.108 = (bf16[8,128,320]{2,1,0:T(8,128)(2,1)}, bf16[8,128,320]{2,1,0:T(8,128)(2,1)}) custom-call(bf16[128,128]{1,0:T(8,128)(2,1)} %shard_map.107.own_ref, bf16[128,128]{1,0:T(8,128)(2,1)} %copy-done.5, bf16[8,8,320,128]{3,2,1,0:T(8,128)(2,1)} %bitcast.18), custom_call_target="tpu_custom_call" | custom-call | flops 1342177280 | bytes 8388608 | tf_op jit(solution)/shard_map/pallas_call | solution.py:219
  168.1 1.5 copy.16
  169.6 2.3 %collective-permute-start.6 = (bf16[8,128,320]{1,2,0:T(8,128)(2,1)S(1)}, bf16[8,128,320]{1,2,0:T(8,128)(2,1)S(1)}, u32[]{:S(2)}, u32[]{:S(2)}) collective-permute-start(bf16[8,128,320]{1,2,0:T(8,128)(2,1)S(1)} %copy.16), channel_id=1, source_target_pairs={{0,16},{16,0},{1,17},{17,1},{2,18},{18,2},{3,19},{19,3},{4,20},{20... | collective-permute-start | bytes 1966088 | tf_op jit(solution)/shard_map/ppermute | solution.py:307
  174.8 5.9 %shard_map.109 = bf16[128,5120]{1,0:T(8,128)(2,1)} custom-call(s32[1]{0:T(128)} %bitcast.c_ref, bf16[8,128,320]{2,1,0:T(8,128)(2,1)} %get-tuple-element.17.own_ref, bf16[8,128,320]{2,1,0:T(8,128)(2,1)} %copy.17.other_ref, f32[128,1]{1,0:T(8,128)} %copy.18.p_ref), custom_call_target="tpu_custom_call" | custom-call | bytes 2621440 | tf_op jit(solution)/shard_map/pallas_call | solution.py:254
  (35 shorter events, 14.9 us)
Async XLA Ops:
  7.2 152.5 %all-gather.2.cloned.1.call-start = ((), (), s32[]{:S(2)}) async-start(), calls=%async_computation.3 | async-start | bytes 5324800 | tf_op jit(solution)/shard_map/all_gather | solution.py:288
  8.1 6.9 %collective-permute-start.4 = (bf16[160,64]{1,0:T(8,128)(2,1)S(1)}, bf16[160,64]{1,0:T(8,128)(2,1)S(1)}, u32[]{:S(2)}, u32[]{:S(2)}) collective-permute-start(bf16[160,64]{1,0:T(8,128)(2,1)S(1)} %bitcast.25), channel_id=1, source_target_pairs={{0,1},{1,0},{2,3},{3,2},{4,5},{5,4},{6,7},{7,6},{8,9},{9,8},{10,11... | collective-permute-start | bytes 61448 | tf_op jit(solution)/shard_map/ppermute | solution.py:282
  15.0 4.7 %collective-permute-start.5 = (bf16[160,128]{1,0:T(8,128)(2,1)S(1)}, bf16[160,128]{1,0:T(8,128)(2,1)S(1)}, u32[]{:S(2)}, u32[]{:S(2)}) collective-permute-start(bf16[160,128]{1,0:T(8,128)(2,1)S(1)} %maximum_select_fusion.1), channel_id=1, source_target_pairs={{0,32},{32,0},{1,33},{33,1},{2,34},{34,2},{3,35},{35,3},{4,36},{36... | collective-permute-start | bytes 122888 | tf_op jit(solution)/shard_map/ppermute | solution.py:286
  21.6 12.2 %collective-permute-start = (bf16[16,160,128]{2,1,0:T(8,128)(2,1)S(1)}, bf16[16,160,128]{2,1,0:T(8,128)(2,1)S(1)}, u32[]{:S(2)}, u32[]{:S(2)}) collective-permute-start(bf16[16,160,128]{2,1,0:T(8,128)(2,1)S(1)} %dynamic-slice_bitcast_fusion), channel_id=1, source_target_pairs={{0,16},{16,0},{1,17},{17,1},{2,18},{18,2},{3,19},{19,3},{4,20},{20... | collective-permute-start | bytes 1966088 | tf_op jit(solution)/shard_map/ppermute | solution.py:279
  33.8 0.8 copy-start.4
  36.7 26.8 %all-to-all-start = ((bf16[16,176,128]{2,1,0:T(8,128)(2,1)}), bf16[16,176,128]{2,1,0:T(8,128)(2,1)S(1)}, u32[]{:S(2)}, u32[]{:S(2)}) async-start(bf16[16,176,128]{2,1,0:T(8,128)(2,1)} %shard_map.104), calls=%async_computation | async-start | bytes 1441792 | tf_op jit(solution)/shard_map/all_to_all | solution.py:292
  63.6 5.2 %copy-start = (bf16[16,176,128]{2,1,0:T(8,128)(2,1)}, bf16[16,176,128]{2,1,0:T(8,128)(2,1)S(1)}, u32[]{:S(2)}) copy-start(bf16[16,176,128]{2,1,0:T(8,128)(2,1)S(1)} %all-to-all-done.g_ref) | copy-start | bytes 2162692
  63.6 49.8 %all-to-all-start.1 = ((bf16[16,64,640]{2,1,0:T(8,128)(2,1)}), bf16[16,64,640]{2,1,0:T(8,128)(2,1)S(1)}, u32[]{:S(2)}, u32[]{:S(2)}) async-start(bf16[16,64,640]{2,1,0:T(8,128)(2,1)} %shard_map.103), calls=%async_computation.1 | async-start | bytes 2621440 | tf_op jit(solution)/shard_map/all_to_all | solution.py:294
  70.8 6.7 %collective-permute-start.1 = (bf16[160,128]{1,0:T(8,128)(2,1)}, bf16[160,128]{1,0:T(8,128)(2,1)S(1)}, u32[]{:S(2)}, u32[]{:S(2)}) collective-permute-start(bf16[160,128]{1,0:T(8,128)(2,1)} %get-tuple-element.14), channel_id=1, source_target_pairs={{0,1},{1,0},{2,3},{3,2},{4,5},{5,4},{6,7},{7,6},{8,9},{9,8},{10,11... | collective-permute-start | bytes 122888 | tf_op jit(solution)/shard_map/ppermute | solution.py:297
  103.2 10.2 %copy-start.3 = (bf16[2560,128]{1,0:T(8,128)(2,1)}, bf16[2560,128]{1,0:T(8,128)(2,1)S(1)}, u32[]{:S(2)}) copy-start(bf16[2560,128]{1,0:T(8,128)(2,1)S(1)} %all_gather.7) | copy-start | bytes 1966084
  103.2 10.2 %collective-permute-start.2 = (bf16[16,160,128]{2,1,0:T(8,128)(2,1)S(1)}, bf16[16,160,128]{2,1,0:T(8,128)(2,1)S(1)}, u32[]{:S(2)}, u32[]{:S(2)}) collective-permute-start(bf16[16,160,128]{2,1,0:T(8,128)(2,1)S(1)} %bitcast.21), channel_id=1, source_target_pairs={{0,16},{16,0},{1,17},{17,1},{2,18},{18,2},{3,19},{19,3},{4,20},{20... | collective-permute-start | bytes 1966088 | tf_op jit(solution)/shard_map/ppermute | solution.py:299
  113.4 0.9 copy-start.8
  113.4 1.3 copy-start.2
  114.7 20.8 %copy-start.6 = (s32[128,1]{0,1:T(1,128)S(1)}, s32[128,1]{0,1:T(1,128)}, u32[]{:S(2)}) copy-start(s32[128,1]{0,1:T(1,128)} %param.14) | copy-start | bytes 1540
  127.6 23.9 %all-to-all-start.2 = ((bf16[16,128,128]{2,1,0:T(8,128)(2,1)}), bf16[16,128,128]{2,1,0:T(8,128)(2,1)S(1)}, u32[]{:S(2)}, u32[]{:S(2)}) async-start(bf16[16,128,128]{2,1,0:T(8,128)(2,1)} %bitcast.23), calls=%async_computation.2 | async-start | bytes 1048576 | tf_op jit(solution)/shard_map/all_to_all | solution.py:303
  151.5 0.8 copy-start.1
  154.1 5.5 %collective-permute-start.3 = (bf16[128,128]{1,0:T(8,128)(2,1)}, bf16[128,128]{1,0:T(8,128)(2,1)S(1)}, u32[]{:S(2)}, u32[]{:S(2)}) collective-permute-start(bf16[128,128]{1,0:T(8,128)(2,1)} %shard_map.107.own_ref), channel_id=1, source_target_pairs={{0,16},{16,0},{1,17},{17,1},{2,18},{18,2},{3,19},{19,3},{4,20},{20... | collective-permute-start | bytes 98312 | tf_op jit(solution)/shard_map/ppermute | solution.py:305
  159.6 0.6 copy-start.5
  168.1 3.8 %copy-start.7 = (f32[128]{0:T(128)S(1)}, f32[128]{0:T(128)}, u32[]{:S(2)}) copy-start(f32[128]{0:T(128)} %param.15) | copy-start | bytes 1540
  169.6 4.0 %collective-permute-start.6 = (bf16[8,128,320]{1,2,0:T(8,128)(2,1)S(1)}, bf16[8,128,320]{1,2,0:T(8,128)(2,1)S(1)}, u32[]{:S(2)}, u32[]{:S(2)}) collective-permute-start(bf16[8,128,320]{1,2,0:T(8,128)(2,1)S(1)} %copy.16), channel_id=1, source_target_pairs={{0,16},{16,0},{1,17},{17,1},{2,18},{18,2},{3,19},{19,3},{4,20},{20... | collective-permute-start | bytes 1966088 | tf_op jit(solution)/shard_map/ppermute | solution.py:307
Sparse Core Ops, SparseCore 0:
  20.6 107.6 all-gather.1

commit v2 on v1

v2 whole, which is shorter than its diff:
```python
import functools

import jax
import jax.numpy as jnp
from jax import lax
from jax.experimental import pallas as pl
from jax.experimental.pallas import tpu as pltpu
from jax.sharding import Mesh, PartitionSpec as P

beta_one = 0.9
beta_two = 0.95
learn_rate = 0.005
decay_rate = 0.1
adam_eps = 1e-08
bias_one = 1.0 - 0.9**50
bias_two = 1.0 - 0.95**50

Z, XL, C, Y, XH = 8, 2, 2, 8, 2
GROUP = Z * XL
EXPERTS = Y * XH
D = 5120
ROWS = 160
COLS = 320
TOK = 128
UNITS = 64
SWAP = ((0, 1), (1, 0))

f32 = jnp.float32
bf16 = jnp.bfloat16


def params(mib):
    return pltpu.CompilerParams(vmem_limit_bytes=mib * 1024 * 1024)


def cost(flops, nbytes):
    return pl.CostEstimate(flops=flops, bytes_accessed=nbytes, transcendentals=0)


def pack_kernel(x_ref, o_ref):
    half = TOK // 2
    for k in range(o_ref.shape[0]):
        at = slice(k * COLS, (k + 1) * COLS)
        o_ref[k, :, :COLS] = x_ref[:half, at]
        o_ref[k, :, COLS:] = x_ref[half:, at]


def pack(tokens):
    steps = 2
    return pl.pallas_call(
        pack_kernel,
        out_shape=jax.ShapeDtypeStruct((GROUP, TOK // 2, 2 * COLS), bf16),
        grid=(steps,),
        in_specs=[pl.BlockSpec((TOK, D // steps), lambda i: (0, i))],
        out_specs=pl.BlockSpec((GROUP // steps, TOK // 2, 2 * COLS), lambda i: (i, 0, 0)),
        compiler_params=params(12),
        cost_estimate=cost(0, 2 * TOK * D * 2),
    )(tokens)


def add_kernel(c_ref, g_ref, r_ref, route_ref, o_ref):
    total = g_ref[:, 0].astype(f32) + r_ref[...].astype(f32)
    o_ref[:, :ROWS] = total.astype(bf16)
    rows = jnp.broadcast_to(route_ref[...].astype(f32), (16, TOK)).astype(bf16)
    for i in range(o_ref.shape[0]):
        o_ref[i, ROWS:] = rows


def add(core, grads, received, route_row):
    n = 8
    return pl.pallas_call(
        add_kernel,
        out_shape=jax.ShapeDtypeStruct((GROUP, ROWS + 16, TOK), bf16),
        grid_spec=pltpu.PrefetchScalarGridSpec(
            num_scalar_prefetch=1,
            grid=(GROUP // n,),
            in_specs=[
                pl.BlockSpec((n, 1, ROWS, 128), lambda i, c: (i, c[0], 0, 0)),
                pl.BlockSpec((n, ROWS, 128), lambda i, c: (i, 0, 0)),
                pl.BlockSpec((1, TOK), lambda i, c: (0, 0)),
            ],
            out_specs=pl.BlockSpec((n, ROWS + 16, TOK), lambda i, c: (i, 0, 0)),
        ),
        compiler_params=params(8),
        cost_estimate=cost(0, 3 * GROUP * ROWS * 256),
    )(core, grads, received, route_row)


def adam_kernel(g_ref, w_ref, m_ref, s_ref, nw_ref, nm_ref, short_ref, route_ref):
    total = g_ref[0, :ROWS].astype(f32)
    for i in range(1, GROUP):
        total = total + g_ref[i, :ROWS].astype(f32)
    weight = w_ref[...]
    moment_new = beta_one * m_ref[...] + (1.0 - beta_one) * total
    second_new = beta_two * s_ref[...] + (1.0 - beta_two) * total * total
    update = moment_new / bias_one / (jnp.sqrt(second_new / bias_two) + adam_eps)
    new_weight = weight - learn_rate * (update + decay_rate * weight)
    nw_ref[...] = new_weight
    nm_ref[...] = moment_new
    short_ref[...] = new_weight.astype(bf16)
    for i in range(GROUP):
        route_ref[i : i + 1, :] = g_ref[i, ROWS : ROWS + 16].astype(f32)[0:1]


def adam(arrived, master, moment, second):
    return pl.pallas_call(
        adam_kernel,
        out_shape=(
            jax.ShapeDtypeStruct((ROWS, 128), f32),
            jax.ShapeDtypeStruct((ROWS, 128), f32),
            jax.ShapeDtypeStruct((ROWS, 128), bf16),
            jax.ShapeDtypeStruct((GROUP, TOK), f32),
        ),
        compiler_params=params(8),
        cost_estimate=cost(0, GROUP * ROWS * 256 + 5 * ROWS * 512),
    )(arrived, master, moment, second)


def partial_kernel(ids_ref, own_ref, other_ref, x_ref, route_ref, o_ref, w_scr, x_scr, r_scr, sems):
    core = ids_ref[0]
    high = ids_ref[1]
    half = TOK // 2
    first = pltpu.make_async_copy(own_ref, w_scr.at[core], sems.at[0])
    second = pltpu.make_async_copy(other_ref, w_scr.at[1 - core], sems.at[1])
    first.start()
    second.start()
    columns = jnp.transpose(route_ref[...])
    for s in range(GROUP):
        x_scr[s * TOK : s * TOK + half, :] = x_ref[s, :, :COLS]
        x_scr[s * TOK + half : (s + 1) * TOK, :] = x_ref[s, :, COLS:]
        r_scr[s * TOK : (s + 1) * TOK, :] = jnp.broadcast_to(columns[:, s : s + 1], (TOK, 128)).astype(bf16)
    first.wait()
    second.wait()
    step = 1024

    def rows(i, carry):
        at = pl.ds(pl.multiple_of(i * step, step), step)
        kept = jnp.zeros((step, 128), bf16)
        route = r_scr[at, :]
        for e in range(0, EXPERTS, 2):
            weights = jnp.concatenate(
                [jnp.concatenate([w_scr[c, e], w_scr[c, e + 1]], axis=1) for c in range(C)], axis=0
            )
            both = jnp.dot(x_scr[at, :], weights, preferred_element_type=f32).astype(bf16)
            kept = jnp.where(route == (e + high).astype(f32).astype(bf16), both[:, :128], kept)
            kept = jnp.where(route == (e + 1 - high).astype(f32).astype(bf16), both[:, 128:], kept)
        o_ref[at, :] = kept
        return carry

    lax.fori_loop(0, GROUP * TOK // step, rows, 0)


def partial_sums(ids, own, other, x, route):
    vmem = pl.BlockSpec(memory_space=pltpu.VMEM)
    anywhere = pl.BlockSpec(memory_space=pl.ANY)
    return pl.pallas_call(
        partial_kernel,
        out_shape=jax.ShapeDtypeStruct((GROUP * TOK, 128), bf16),
        in_specs=[pl.BlockSpec(memory_space=pltpu.SMEM), anywhere, anywhere, vmem, vmem],
        out_specs=vmem,
        scratch_shapes=[
            pltpu.VMEM((C, EXPERTS, ROWS, 128), bf16),
            pltpu.VMEM((GROUP * TOK, COLS), bf16),
            pltpu.VMEM((GROUP * TOK, 128), bf16),
            pltpu.SemaphoreType.DMA((2,)),
        ],
        compiler_params=params(20),
        cost_estimate=cost(2 * GROUP * TOK * COLS * EXPERTS * 128, 4 * 1024 * 1024),
    )(ids, own, other, x, route)


def finish_kernel(p_ref, route_ref, prob_ref, d_ref, o_ref, w_scr, h_scr, prob_scr, sems):
    step = pl.program_id(0)
    n = Z // pl.num_programs(0)

    def weights(z):
        return pltpu.make_async_copy(d_ref.at[z], w_scr.at[z], sems.at[z])

    @pl.when(step == 0)
    def _():
        for z in range(Z):
            weights(z).start()
        total = p_ref[0].astype(f32)
        for i in range(1, GROUP):
            total = total + p_ref[i].astype(f32)
        gate = total[:, :UNITS]
        up = total[:, UNITS:]
        hidden = gate * jax.nn.sigmoid(gate) * up
        rows = [jnp.broadcast_to(r, (4, TOK)) for r in (route_ref[...].astype(f32), prob_ref[...])]
        columns = jnp.transpose(jnp.concatenate(rows, axis=0))
        route = jnp.broadcast_to(columns[:, 0:1], (TOK, UNITS))
        prob_scr[...] = jnp.broadcast_to(columns[:, 4:5], (TOK, 128))
        for j in range(XH):
            for y in range(Y):
                at = (j * Y + y) * UNITS
                h_scr[:, at : at + UNITS] = jnp.where(route == 2.0 * y + j, hidden, 0.0).astype(bf16)

    prob = jnp.concatenate([prob_scr[...]] * 5, axis=1)
    split = Y * UNITS
    for k in range(n):
        z = step * n + k
        weights(z).wait()
        outs = []
        for c in range(C):
            block = w_scr[z, :, c].reshape(split, 2 * COLS)
            low = jnp.dot(h_scr[:, :split], block[:, :COLS], preferred_element_type=f32)
            wide = jnp.dot(h_scr[:, split:], block[:, COLS - UNITS :], preferred_element_type=f32)
            outs.append((low + wide[:, UNITS:]).astype(bf16))
        even, odd = outs
        blocks = [even[:, :ROWS], odd[:, :ROWS], even[:, ROWS:], odd[:, ROWS:]]
        whole = jnp.concatenate(blocks, axis=1).astype(f32)
        o_ref[:, k * 2 * COLS : (k + 1) * 2 * COLS] = (prob * whole).astype(bf16)


def finish(parts, route_row, prob_row, down):
    steps = 4
    return pl.pallas_call(
        finish_kernel,
        out_shape=jax.ShapeDtypeStruct((TOK, D), bf16),
        grid=(steps,),
        in_specs=[
            pl.BlockSpec((GROUP, TOK, 128), lambda i: (0, 0, 0)),
            pl.BlockSpec((1, TOK), lambda i: (0, 0)),
            pl.BlockSpec((1, TOK), lambda i: (0, 0)),
            pl.BlockSpec(memory_space=pl.ANY),
        ],
        out_specs=pl.BlockSpec((TOK, D // steps), lambda i: (0, i)),
        scratch_shapes=[
            pltpu.VMEM((Z, Y, C, UNITS, 2 * COLS), bf16),
            pltpu.VMEM((TOK, EXPERTS * UNITS), bf16),
            pltpu.VMEM((TOK, 128), f32),
            pltpu.SemaphoreType.DMA((Z,)),
        ],
        compiler_params=params(52),
        cost_estimate=cost(2 * TOK * EXPERTS * UNITS * D, 12 * 1024 * 1024),
    )(parts, route_row, prob_row, down)


def shards(grad_parts, master, moment, second, down_weight, tokens, routes, probs):
    core = lax.axis_index("c")
    low = lax.axis_index("xl")
    high = lax.axis_index("xh")
    core_id = core.reshape(1).astype(jnp.int32)
    group = ("z", "xl")

    grads = grad_parts.reshape(GROUP, C, ROWS, 128)
    sent = lax.dynamic_index_in_dim(grads, 1 - core, axis=1, keepdims=False)
    received = lax.ppermute(sent, "c", SWAP)

    down = jnp.broadcast_to(down_weight[0].T[None], (XH * XL, UNITS, ROWS))
    four = lax.all_to_all(down, ("xh", "xl"), 0, 0, tiled=True)
    pair = jnp.transpose(four, (1, 0, 2)).reshape(UNITS, 2 * COLS)
    pair, received = lax.optimization_barrier((pair, received))
    down_all = lax.all_gather(pair, ("z", "y", "c"), axis=0, tiled=False)
    down_all = down_all.reshape(Z, Y, C, UNITS, 2 * COLS)
    chunk = add(core_id, grads, received, routes.reshape(1, TOK))
    arrived = lax.all_to_all(chunk, group, 0, 0, tiled=True)

    new_master, new_moment, short, route_all = adam(arrived, master[0], moment[0], second[0])
    pair_short = jnp.concatenate([short, lax.ppermute(short, "xh", SWAP)], axis=0)
    tokens, _ = lax.optimization_barrier((tokens, short))
    packed, pair_short = lax.optimization_barrier((pack(tokens), pair_short))
    columns = lax.all_to_all(packed, group, 0, 0, tiled=True)
    own = lax.all_gather(pair_short, "y", axis=0, tiled=True).reshape(EXPERTS, ROWS, 128)
    other = lax.ppermute(own, "c", SWAP)

    ids = jnp.stack([core, high]).astype(jnp.int32)
    parts = partial_sums(ids, own, other, columns, route_all)
    parts = lax.all_to_all(parts.reshape(GROUP, TOK, 128), group, 0, 0, tiled=True)
    mixed = finish(parts, routes.reshape(1, TOK), probs.reshape(1, TOK), down_all)
    return new_master[None], new_moment[None], mixed


def solution(mesh):
    fine = Mesh(mesh.devices.reshape(Z, XL, C, Y, XH), ("z", "xl", "c", "y", "xh"))
    dp, expert = ("z", "xl", "c"), ("y", "xh")
    both = dp + expert
    in_specs = (
        P(expert, dp, None, None),
        P(expert, dp, None),
        P(expert, dp, None),
        P(expert, dp, None),
        P(expert, dp, None),
        P(both, None),
        P(both, None),
        P(both),
    )
    out_specs = (P(expert, dp, None), P(expert, dp, None), P(both, None))
    return jax.shard_map(shards, mesh=fine, in_specs=in_specs, out_specs=out_specs, check_vma=False)
```

time: 189 us -> 150 us (0.79)
  blocking collectives: 24.9 us -> 85.5 us
  waiting for transfers between devices: 40.8 us -> 3.59 us
  starting transfers between devices: 57.6 us -> 28.1 us
  Pallas kernels: 38.3 us -> 15.1 us
  local copies, waits for them, and re-layouts: 9.68 us -> 2.91 us
  other arithmetic: 2.15 us -> 0.08 us
    all_to_all x0 -> x3, blocking collectives: none -> 62.6 us  [the longest x1 28.5 us: shards(): lax.all_to_all(parts.reshape(GROUP, TOK, 128), group, 0, 0, tiled=True)]
    all_to_all x2 -> x0, waiting for transfers between devices: 30.8 us -> none  [the longest x1 15.5 us: shards(): arrived = lax.all_to_all(chunk, group, 0, 0, tiled=True)]
    ppermute x4 -> x0, starting transfers between devices: 15.5 us -> none  [the longest x1 5.48 us: shards(): beside = lax.ppermute(down, 'xh', SWAP)]
    all_to_all x2 -> x0, starting transfers between devices: 13.6 us -> none  [the longest x1 7.86 us: shards(): lax.all_to_all(parts.reshape(GROUP, TOK, 128), group, 0, 0, tiled=True)]
    pallas_call x3 -> x1, Pallas kernels: 15.6 us -> 6.39 us  [finish(): pl.pallas_call(finish_kernel, out_shape=jax.ShapeDtypeStruct((TOK, D), bf...]
    pallas_call x1, Pallas kernels: 13 us -> 6.29 us  [partial_sums(): pl.pallas_call(partial_kernel, out_shape=jax.ShapeDtypeStruct((GROUP * TO...]
    unnamed x20 -> x14, local copies, waits for them, and re-layouts: 5.12 us -> 0.04 us
    ppermute x4 -> x0, waiting for transfers between devices: 4.79 us -> none  [the longest x1 1.4 us: shards(): beside = lax.ppermute(pair, 'xl', SWAP)]
  transfers between devices with their start and end apart: 11 -> 5, of which waited for: 9 -> 3; matrix products, arithmetic and copies ran while one was open for 2% -> 1% of each run, Pallas kernels for 13% -> 6%
where the time goes in v2:
time: 150 us
  blocking collectives  85.5 us (57%)
  starting transfers between devices  28.1 us (19%)
  Pallas kernels  15.1 us (10%)
  between operations  14.2 us (9%)
  waiting for transfers between devices  3.59 us (2%)
  local copies, waits for them, and re-layouts  2.91 us (2%)
    all_to_all x1, blocking collectives, shards(): lax.all_to_all(parts.reshape(GROUP, TOK, 128), group, 0, 0, tiled=True)  28.5 us
    all_to_all x1, blocking collectives, shards(): arrived = lax.all_to_all(chunk, group, 0, 0, tiled=True)  26.5 us
    all_gather x1, blocking collectives, shards(): lax.all_gather(pair_short, 'y', axis=0, tiled=True)  22.9 us
    ppermute x1, starting transfers between devices, shards(): other = lax.ppermute(own, 'c', SWAP)  11.3 us
    ppermute x1, starting transfers between devices, shards(): received = lax.ppermute(sent, 'c', SWAP)  8.79 us
    all_to_all x1, blocking collectives, shards(): four = lax.all_to_all(down, ('xh', 'xl'), 0, 0, tiled=True)  7.51 us
    pallas_call x1, Pallas kernels, finish(): pl.pallas_call(finish_kernel, out_shape=jax.ShapeDtypeStruct((TOK, D), bf...  6.39 us
    pallas_call x1, Pallas kernels, partial_sums(): pl.pallas_call(partial_kernel, out_shape=jax.ShapeDtypeStruct((GROUP * TO...  6.29 us
  transfers between devices with their start and end apart: 5, of which 3 were waited for; matrix products, arithmetic and copies ran while one was open for 1% of the time, Pallas kernels for 6%

profile of v2, /device:TPU:1, one launch (start us, length us, event | category | flops | bytes accessed | tf_op | source)
XLA Modules:
  0.0 149.5 jit_solution(6127302471442258977)
XLA Ops:
  7.2 0.0 all-gather.3.cloned.1.call-start
  7.2 1.2 dynamic-slice_bitcast_fusion
  8.5 8.8 %collective-permute-start = (bf16[16,160,128]{2,1,0:T(8,128)(2,1)S(1)}, bf16[16,160,128]{2,1,0:T(8,128)(2,1)S(1)}, u32[]{:S(2)}, u32[]{:S(2)}) collective-permute-start(bf16[16,160,128]{2,1,0:T(8,128)(2,1)S(1)} %dynamic-slice_bitcast_fusion), channel_id=1, source_target_pairs={{0,16},{16,0},{1,17},{17,1},{2,18},{18,2},{3,19},{19,3},{4,20},{20... | collective-permute-start | bytes 1966088 | tf_op jit(solution)/shard_map/ppermute | solution.py:248
  17.3 0.8 broadcast_in_dim.12
  18.0 7.5 %all_to_all.20 = bf16[4,64,160]{2,1,0:T(8,128)(2,1)S(1)} all-to-all(bf16[4,64,160]{2,1,0:T(8,128)(2,1)S(1)} %broadcast_in_dim.12), channel_id=1, replica_groups=mesh['z'=8,'xl'=2,'c'=2,'y'=8,'xh'=2] {'xh','xl'}, dimensions={0} | all-to-all | bytes 163840 | tf_op jit(solution)/shard_map/all_to_all | solution.py:251
  25.6 0.1 copy.11
  25.7 0.8 reshape.34
  26.4 0.0 all-gather.3.cloned.1.call-update
  26.5 0.0 copy-start.3
  26.5 0.3 shard_map.103
  26.8 26.5 %all_to_all.21.g_ref = bf16[16,176,128]{2,1,0:T(8,128)(2,1)S(1)} all-to-all(bf16[16,176,128]{2,1,0:T(8,128)(2,1)S(1)} %shard_map.103), channel_id=1, replica_groups=mesh['z'=8,'xl'=2,'c'=2,'y'=8,'xh'=2] {'z','xl'}, dimensions={0} | all-to-all | bytes 1441792 | tf_op jit(solution)/shard_map/all_to_all | solution.py:257
  53.4 0.8 shard_map.104
  54.2 3.5 %collective-permute-start.1 = (bf16[160,128]{1,0:T(8,128)(2,1)S(1)}, bf16[160,128]{1,0:T(8,128)(2,1)S(1)}, u32[]{:S(2)}, u32[]{:S(2)}) collective-permute-start(bf16[160,128]{1,0:T(8,128)(2,1)S(1)} %get-tuple-element.15), channel_id=1, source_target_pairs={{0,1},{1,0},{2,3},{3,2},{4,5},{5,4},{6,7},{7,6},{8,9},{9,8},{10,11... | collective-permute-start | bytes 122888 | tf_op jit(solution)/shard_map/ppermute | solution.py:260
  57.7 1.4 shard_map.105
  59.0 1.4 collective-permute-done.1
  60.4 4.5 %all-to-all-start.2 = ((bf16[16,64,640]{2,1,0:T(8,128)(2,1)}), bf16[16,64,640]{2,1,0:T(8,128)(2,1)S(1)}, u32[]{:S(2)}, u32[]{:S(2)}) async-start(bf16[16,64,640]{2,1,0:T(8,128)(2,1)} %shard_map.105), calls=%async_computation.2 | async-start | bytes 2621440 | tf_op jit(solution)/shard_map/all_to_all | solution.py:263
  64.9 22.9 %all_gather.9 = bf16[2560,128]{1,0:T(8,128)(2,1)S(1)} all-gather(bf16[320,128]{1,0:T(8,128)(2,1)S(1)} %pad_maximum_fusion), channel_id=1, replica_groups=mesh['z'=8,'xl'=2,'c'=2,'y'=8,'xh'=2] {'y'}, dimensions={0}, use_global_device_ids=true | all-gather | bytes 737280 | tf_op jit(solution)/shard_map/all_gather | solution.py:264
  87.8 11.3 %collective-permute-start.2 = (bf16[16,160,128]{2,1,0:T(8,128)(2,1)S(1)}, bf16[16,160,128]{2,1,0:T(8,128)(2,1)S(1)}, u32[]{:S(2)}, u32[]{:S(2)}) collective-permute-start(bf16[16,160,128]{2,1,0:T(8,128)(2,1)S(1)} %bitcast.21), channel_id=1, source_target_pairs={{0,16},{16,0},{1,17},{17,1},{2,18},{18,2},{3,19},{19,3},{4,20},{20... | collective-permute-start | bytes 1966088 | tf_op jit(solution)/shard_map/ppermute | solution.py:265
  99.2 0.1 pad_add_fusion.ids_ref
  99.2 1.7 %collective-permute-done.2.other_ref = bf16[16,160,128]{2,1,0:T(8,128)(2,1)S(1)} collective-permute-done((bf16[16,160,128]{2,1,0:T(8,128)(2,1)S(1)}, bf16[16,160,128]{2,1,0:T(8,128)(2,1)S(1)}, u32[]{:S(2)}, u32[]{:S(2)}) %collective-permute-start.2) | collective-permute-done | bytes 655392 | tf_op jit(solution)/shard_map/ppermute | solution.py:265
  101.0 6.3 %shard_map.106 = bf16[2048,128]{1,0:T(8,128)(2,1)S(1)} custom-call(s32[2]{0:T(128)S(1)} %pad_add_fusion.ids_ref, bf16[16,160,128]{2,1,0:T(8,128)(2,1)S(1)} %bitcast.22, bf16[16,160,128]{2,1,0:T(8,128)(2,1)S(1)} %collective-permute-done.2.other_ref, bf16[16,64,640]{2,1,0:T(8,128)(2,1)S(1)} %all-to-all-done.2.x_ref, f32[16,128]{1,0:T(8,128)S(1)} %get-tuple-element.19.route_ref), custom_call_target="tpu_custom_call" | custom-call | flops 2684354560 | bytes 4194304 | tf_op jit(solution)/shard_map/pallas_call | solution.py:156
  107.3 28.5 %all_to_all.22.p_ref = bf16[16,128,128]{2,1,0:T(8,128)(2,1)S(1)} all-to-all(bf16[16,128,128]{2,1,0:T(8,128)(2,1)S(1)} %bitcast.23), channel_id=1, replica_groups=mesh['z'=8,'xl'=2,'c'=2,'y'=8,'xh'=2] {'z','xl'}, dimensions={0} | all-to-all | bytes 1048576 | tf_op jit(solution)/shard_map/all_to_all | solution.py:269
  135.8 0.5 all-gather.3.cloned.1.call-done
  136.3 6.4 %shard_map.107 = bf16[128,5120]{1,0:T(8,128)(2,1)} custom-call(bf16[16,128,128]{2,1,0:T(8,128)(2,1)S(1)} %all_to_all.22.p_ref, s32[1,128]{1,0:T(1,128)S(1)} %bitcast.28, f32[1,128]{1,0:T(1,128)S(1)} %bitcast.29, bf16[8,8,2,64,640]{4,3,2,1,0:T(8,128)(2,1)} %bitcast.30), custom_call_target="tpu_custom_call" | custom-call | flops 1342177280 | bytes 12582912 | tf_op jit(solution)/shard_map/pallas_call | solution.py:217
  (16 shorter events, 0.0 us)
Async XLA Ops:
  7.2 19.3 %copy-start = (bf16[1,1,5120,128]{3,2,1,0:T(8,128)(2,1)S(1)}, bf16[1,1,5120,128]{3,2,1,0:T(8,128)(2,1)}, u32[]{:S(2)}) copy-start(bf16[1,1,5120,128]{3,2,1,0:T(8,128)(2,1)} %param.8) | copy-start | bytes 3932164
  7.2 19.3 %copy-start.5 = (s32[128,1]{0,1:T(1,128)S(1)}, s32[128,1]{0,1:T(1,128)}, u32[]{:S(2)}) copy-start(s32[128,1]{0,1:T(1,128)} %param.14) | copy-start | bytes 1540
  7.2 129.1 %all-gather.3.cloned.1.call-start = ((), (), s32[]{:S(2)}) async-start(), calls=%async_computation.4 | async-start | bytes 10567680 | tf_op jit(solution)/shard_map/all_gather | solution.py:254
  8.5 18.0 %collective-permute-start = (bf16[16,160,128]{2,1,0:T(8,128)(2,1)S(1)}, bf16[16,160,128]{2,1,0:T(8,128)(2,1)S(1)}, u32[]{:S(2)}, u32[]{:S(2)}) collective-permute-start(bf16[16,160,128]{2,1,0:T(8,128)(2,1)S(1)} %dynamic-slice_bitcast_fusion), channel_id=1, source_target_pairs={{0,16},{16,0},{1,17},{17,1},{2,18},{18,2},{3,19},{19,3},{4,20},{20... | collective-permute-start | bytes 1966088 | tf_op jit(solution)/shard_map/ppermute | solution.py:248
  26.5 26.9 %copy-start.3 = (f32[1,160,128]{2,1,0:T(8,128)S(1)}, f32[1,160,128]{2,1,0:T(8,128)}, u32[]{:S(2)}) copy-start(f32[1,160,128]{2,1,0:T(8,128)} %param.10) | copy-start | bytes 245764
  26.5 26.9 %copy-start.4 = (f32[1,160,128]{2,1,0:T(8,128)S(1)}, f32[1,160,128]{2,1,0:T(8,128)}, u32[]{:S(2)}) copy-start(f32[1,160,128]{2,1,0:T(8,128)} %param.11) | copy-start | bytes 245764
  26.8 26.6 %copy-start.2 = (f32[1,160,128]{2,1,0:T(8,128)S(1)}, f32[1,160,128]{2,1,0:T(8,128)}, u32[]{:S(2)}) copy-start(f32[1,160,128]{2,1,0:T(8,128)} %param.9) | copy-start | bytes 245764
  26.8 30.9 %copy-start.1 = (bf16[128,5120]{1,0:T(8,128)(2,1)S(1)}, bf16[128,5120]{1,0:T(8,128)(2,1)}, u32[]{:S(2)}) copy-start(bf16[128,5120]{1,0:T(8,128)(2,1)} %x_ref) | copy-start | bytes 3932164
  54.2 6.2 %collective-permute-start.1 = (bf16[160,128]{1,0:T(8,128)(2,1)S(1)}, bf16[160,128]{1,0:T(8,128)(2,1)S(1)}, u32[]{:S(2)}, u32[]{:S(2)}) collective-permute-start(bf16[160,128]{1,0:T(8,128)(2,1)S(1)} %get-tuple-element.15), channel_id=1, source_target_pairs={{0,1},{1,0},{2,3},{3,2},{4,5},{5,4},{6,7},{7,6},{8,9},{9,8},{10,11... | collective-permute-start | bytes 122888 | tf_op jit(solution)/shard_map/ppermute | solution.py:260
  60.4 40.6 %all-to-all-start.2 = ((bf16[16,64,640]{2,1,0:T(8,128)(2,1)}), bf16[16,64,640]{2,1,0:T(8,128)(2,1)S(1)}, u32[]{:S(2)}, u32[]{:S(2)}) async-start(bf16[16,64,640]{2,1,0:T(8,128)(2,1)} %shard_map.105), calls=%async_computation.2 | async-start | bytes 2621440 | tf_op jit(solution)/shard_map/all_to_all | solution.py:263
  87.8 13.2 %collective-permute-start.2 = (bf16[16,160,128]{2,1,0:T(8,128)(2,1)S(1)}, bf16[16,160,128]{2,1,0:T(8,128)(2,1)S(1)}, u32[]{:S(2)}, u32[]{:S(2)}) collective-permute-start(bf16[16,160,128]{2,1,0:T(8,128)(2,1)S(1)} %bitcast.21), channel_id=1, source_target_pairs={{0,16},{16,0},{1,17},{17,1},{2,18},{18,2},{3,19},{19,3},{4,20},{20... | collective-permute-start | bytes 1966088 | tf_op jit(solution)/shard_map/ppermute | solution.py:265
  101.0 35.3 %copy-start.6 = (f32[128]{0:T(128)S(1)}, f32[128]{0:T(128)}, u32[]{:S(2)}) copy-start(f32[128]{0:T(128)} %param.15) | copy-start | bytes 1540
Sparse Core Ops, SparseCore 0:
  26.6 109.6 all-gather.2

commit v3 on v2

--- a/solution.py
+++ b/solution.py
@@ -38,21 +38,23 @@
 
 
 def pack_kernel(x_ref, o_ref):
-    half = TOK // 2
+    quarter = TOK // 4
     for k in range(o_ref.shape[0]):
-        at = slice(k * COLS, (k + 1) * COLS)
-        o_ref[k, :, :COLS] = x_ref[:half, at]
-        o_ref[k, :, COLS:] = x_ref[half:, at]
+        for c in range(C):
+            at = slice((k * C + c) * ROWS, (k * C + c + 1) * ROWS)
+            part = x_ref[:, at]
+            groups = [part[q * quarter : (q + 1) * quarter] for q in range(4)]
+            o_ref[k, c] = jnp.concatenate(groups, axis=1)
 
 
 def pack(tokens):
     steps = 2
     return pl.pallas_call(
         pack_kernel,
-        out_shape=jax.ShapeDtypeStruct((GROUP, TOK // 2, 2 * COLS), bf16),
+        out_shape=jax.ShapeDtypeStruct((GROUP, C, TOK // 4, 4 * ROWS), bf16),
         grid=(steps,),
         in_specs=[pl.BlockSpec((TOK, D // steps), lambda i: (0, i))],
-        out_specs=pl.BlockSpec((GROUP // steps, TOK // 2, 2 * COLS), lambda i: (i, 0, 0)),
+        out_specs=pl.BlockSpec((GROUP // steps, C, TOK // 4, 4 * ROWS), lambda i: (i, 0, 0, 0)),
         compiler_params=params(12),
         cost_estimate=cost(0, 2 * TOK * D * 2),
     )(tokens)
@@ -116,57 +118,76 @@
     )(arrived, master, moment, second)
 
 
-def partial_kernel(ids_ref, own_ref, other_ref, x_ref, route_ref, o_ref, w_scr, x_scr, r_scr, sems):
-    core = ids_ref[0]
-    high = ids_ref[1]
-    half = TOK // 2
-    first = pltpu.make_async_copy(own_ref, w_scr.at[core], sems.at[0])
-    second = pltpu.make_async_copy(other_ref, w_scr.at[1 - core], sems.at[1])
-    first.start()
-    second.start()
+def select_sums(x_ref, core, w_ref, high, x_scr, route_ref, start, store):
+    quarter = TOK // 4
+    for s in range(GROUP):
+        block = x_ref[s, core]
+        for q in range(4):
+            at = s * TOK + q * quarter
+            x_scr[at : at + quarter, :] = block[:, q * ROWS : (q + 1) * ROWS]
+    step = 1024
+
+    def rows(i, carry):
+        at = pl.ds(pl.multiple_of(i * step, step), step)
+        kept = jnp.zeros((step, 128), f32)
+        route = route_ref[at, :].astype(f32)
+        for e in range(0, EXPERTS, 2):
+            weights = jnp.concatenate([w_ref[e], w_ref[e + 1]], axis=1)
+            both = jnp.dot(x_scr[at, :], weights, preferred_element_type=f32)
+            kept = jnp.where(route == (e + high).astype(f32), both[:, :128], kept)
+            kept = jnp.where(route == (e + 1 - high).astype(f32), both[:, 128:], kept)
+        store(at, kept if start is None else kept + start[at, :])
+        return carry
+
+    lax.fori_loop(0, GROUP * TOK // step, rows, 0)
+
+
+def first_kernel(ids_ref, w_ref, x_ref, route_ref, o_ref, spread_ref, x_scr):
     columns = jnp.transpose(route_ref[...])
     for s in range(GROUP):
-        x_scr[s * TOK : s * TOK + half, :] = x_ref[s, :, :COLS]
-        x_scr[s * TOK + half : (s + 1) * TOK, :] = x_ref[s, :, COLS:]
-        r_scr[s * TOK : (s + 1) * TOK, :] = jnp.broadcast_to(columns[:, s : s + 1], (TOK, 128)).astype(bf16)
-    first.wait()
-    second.wait()
-    step = 1024
-
-    def rows(i, carry):
-        at = pl.ds(pl.multiple_of(i * step, step), step)
-        kept = jnp.zeros((step, 128), bf16)
-        route = r_scr[at, :]
-        for e in range(0, EXPERTS, 2):
-            weights = jnp.concatenate(
-                [jnp.concatenate([w_scr[c, e], w_scr[c, e + 1]], axis=1) for c in range(C)], axis=0
-            )
-            both = jnp.dot(x_scr[at, :], weights, preferred_element_type=f32).astype(bf16)
-            kept = jnp.where(route == (e + high).astype(f32).astype(bf16), both[:, :128], kept)
-            kept = jnp.where(route == (e + 1 - high).astype(f32).astype(bf16), both[:, 128:], kept)
-        o_ref[at, :] = kept
-        return carry
-
-    lax.fori_loop(0, GROUP * TOK // step, rows, 0)
-
-
-def partial_sums(ids, own, other, x, route):
+        wide = jnp.broadcast_to(columns[:, s : s + 1], (TOK, 128))
+        spread_ref[s * TOK : (s + 1) * TOK, :] = wide.astype(bf16)
+
+    def store(at, value):
+        o_ref[at, :] = value
+
+    select_sums(x_ref, ids_ref[0], w_ref, ids_ref[1], x_scr, spread_ref, None, store)
+
+
+def second_kernel(ids_ref, w_ref, x_ref, spread_ref, p_ref, o_ref, x_scr):
+    def store(at, value):
+        o_ref[at, :] = value.astype(bf16)
+
+    select_sums(x_ref, 1 - ids_ref[0], w_ref, ids_ref[1], x_scr, spread_ref, p_ref, store)
+
+
+def first_sums(ids, weights, x, route):
     vmem = pl.BlockSpec(memory_space=pltpu.VMEM)
-    anywhere = pl.BlockSpec(memory_space=pl.ANY)
-    return pl.pallas_call(
-        partial_kernel,
+    return pl.pallas_call(
+        first_kernel,
+        out_shape=(
+            jax.ShapeDtypeStruct((GROUP * TOK, 128), f32),
+            jax.ShapeDtypeStruct((GROUP * TOK, 128), bf16),
+        ),
+        in_specs=[pl.BlockSpec(memory_space=pltpu.SMEM), vmem, vmem, vmem],
+        out_specs=(vmem, vmem),
+        scratch_shapes=[pltpu.VMEM((GROUP * TOK, ROWS), bf16)],
+        compiler_params=params(20),
+        cost_estimate=cost(2 * GROUP * TOK * ROWS * EXPERTS * 128, 4 * 1024 * 1024),
+    )(ids, weights, x, route)
+
+
+def second_sums(ids, weights, x, spread, parts):
+    vmem = pl.BlockSpec(memory_space=pltpu.VMEM)
+    return pl.pallas_call(
+        second_kernel,
         out_shape=jax.ShapeDtypeStruct((GROUP * TOK, 128), bf16),
-        in_specs=[pl.BlockSpec(memory_space=pltpu.SMEM), anywhere, anywhere, vmem, vmem],
+        in_specs=[pl.BlockSpec(memory_space=pltpu.SMEM)] + [vmem] * 4,
         out_specs=vmem,
-        scratch_shapes=[
-            pltpu.VMEM((C, EXPERTS, ROWS, 128), bf16),
-            pltpu.VMEM((GROUP * TOK, COLS), bf16),
-            pltpu.VMEM((GROUP * TOK, 128), bf16),
-            pltpu.SemaphoreType.DMA((2,)),
-        ],
+        scratch_shapes=[pltpu.VMEM((GROUP * TOK, ROWS), bf16)],
         compiler_params=params(20),
-        cost_estimate=cost(2 * GROUP * TOK * COLS * EXPERTS * 128, 4 * 1024 * 1024),
-    )(ids, own, other, x, route)
+        cost_estimate=cost(2 * GROUP * TOK * ROWS * EXPERTS * 128, 4 * 1024 * 1024),
+    )(ids, weights, x, spread, parts)
 
 
 def finish_kernel(p_ref, route_ref, prob_ref, d_ref, o_ref, w_scr, h_scr, prob_scr, sems):
@@ -255,17 +276,17 @@
     down_all = down_all.reshape(Z, Y, C, UNITS, 2 * COLS)
     chunk = add(core_id, grads, received, routes.reshape(1, TOK))
     arrived = lax.all_to_all(chunk, group, 0, 0, tiled=True)
+    packed, arrived = lax.optimization_barrier((pack(tokens), arrived))
+    columns = lax.all_to_all(packed, group, 0, 0, tiled=True)
 
     new_master, new_moment, short, route_all = adam(arrived, master[0], moment[0], second[0])
     pair_short = jnp.concatenate([short, lax.ppermute(short, "xh", SWAP)], axis=0)
-    tokens, _ = lax.optimization_barrier((tokens, short))
-    packed, pair_short = lax.optimization_barrier((pack(tokens), pair_short))
-    columns = lax.all_to_all(packed, group, 0, 0, tiled=True)
     own = lax.all_gather(pair_short, "y", axis=0, tiled=True).reshape(EXPERTS, ROWS, 128)
     other = lax.ppermute(own, "c", SWAP)
 
     ids = jnp.stack([core, high]).astype(jnp.int32)
-    parts = partial_sums(ids, own, other, columns, route_all)
+    parts, spread = first_sums(ids, own, columns, route_all)
+    parts = second_sums(ids, other, columns, spread, parts)
     parts = lax.all_to_all(parts.reshape(GROUP, TOK, 128), group, 0, 0, tiled=True)
     mixed = finish(parts, routes.reshape(1, TOK), probs.reshape(1, TOK), down_all)
     return new_master[None], new_moment[None], mixed

time: 150 us -> 145 us (0.967)
  blocking collectives: 85.5 us -> 57.2 us
  waiting for transfers between devices: 3.59 us -> 20.4 us
  starting transfers between devices: 28.1 us -> 33.3 us
  Pallas kernels: 15.1 us -> 16.9 us
    all_to_all x1 -> x0, blocking collectives: 26.5 us -> none  [shards(): arrived = lax.all_to_all(chunk, group, 0, 0, tiled=True)]
    all_to_all x0 -> x1, waiting for transfers between devices: none -> 17.6 us  [shards(): arrived = lax.all_to_all(chunk, group, 0, 0, tiled=True)]
    all_to_all x0 -> x1, starting transfers between devices: none -> 6.13 us  [shards(): arrived = lax.all_to_all(chunk, group, 0, 0, tiled=True)]
    all_to_all x1, blocking collectives: 28.5 us -> 25.8 us  [shards(): lax.all_to_all(parts.reshape(GROUP, TOK, 128), group, 0, 0, tiled=True)]
    ppermute x1, starting transfers between devices: 11.3 us -> 9.02 us  [shards(): other = lax.ppermute(own, 'c', SWAP)]
    ppermute x1, waiting for transfers between devices: 1.73 us -> 0.01 us  [shards(): other = lax.ppermute(own, 'c', SWAP)]
    pallas_call x2 -> x3, Pallas kernels: 7.66 us -> 8.7 us  [the longest x1 3.7 us: first_sums(): pl.pallas_call(first_kernel, out_shape=(jax.ShapeDtypeStruct((GROUP * TOK...]
  transfers between devices with their start and end apart: 5 -> 6, of which waited for: 3 -> 2; matrix products, arithmetic and copies ran while one was open for 1% -> 1% of each run, Pallas kernels for 6% -> 7%
where the time goes in v3:
time: 145 us
  blocking collectives  57.2 us (39%)
  starting transfers between devices  33.3 us (23%)
  waiting for transfers between devices  20.4 us (14%)
  Pallas kernels  16.9 us (12%)
  between operations  14.2 us (10%)
  local copies, waits for them, and re-layouts  2.89 us (2%)
    all_to_all x1, blocking collectives, shards(): lax.all_to_all(parts.reshape(GROUP, TOK, 128), group, 0, 0, tiled=True)  25.8 us
    all_gather x1, blocking collectives, shards(): lax.all_gather(pair_short, 'y', axis=0, tiled=True)  23.8 us
    all_to_all x1, waiting for transfers between devices, shards(): arrived = lax.all_to_all(chunk, group, 0, 0, tiled=True)  17.6 us
    ppermute x1, starting transfers between devices, shards(): other = lax.ppermute(own, 'c', SWAP)  9.02 us
    ppermute x1, starting transfers between devices, shards(): received = lax.ppermute(sent, 'c', SWAP)  8.79 us
    all_to_all x1, blocking collectives, shards(): four = lax.all_to_all(down, ('xh', 'xl'), 0, 0, tiled=True)  7.51 us
    pallas_call x1, Pallas kernels, finish(): pl.pallas_call(finish_kernel, out_shape=jax.ShapeDtypeStruct((TOK, D), bf...  6.39 us
    all_to_all x1, starting transfers between devices, shards(): arrived = lax.all_to_all(chunk, group, 0, 0, tiled=True)  6.13 us
  transfers between devices with their start and end apart: 6, of which 2 were waited for; matrix products, arithmetic and copies ran while one was open for 1% of the time, Pallas kernels for 7%

profile of v3, /device:TPU:1, one launch (start us, length us, event | category | flops | bytes accessed | tf_op | source)
XLA Modules:
  0.0 144.9 jit_solution(4823557338593662658)
XLA Ops:
  7.2 0.0 all-gather.3.cloned.1.call-start
  7.2 1.2 dynamic-slice_bitcast_fusion
  8.5 8.8 %collective-permute-start = (bf16[16,160,128]{2,1,0:T(8,128)(2,1)S(1)}, bf16[16,160,128]{2,1,0:T(8,128)(2,1)S(1)}, u32[]{:S(2)}, u32[]{:S(2)}) collective-permute-start(bf16[16,160,128]{2,1,0:T(8,128)(2,1)S(1)} %dynamic-slice_bitcast_fusion), channel_id=1, source_target_pairs={{0,16},{16,0},{1,17},{17,1},{2,18},{18,2},{3,19},{19,3},{4,20},{20... | collective-permute-start | bytes 1966088 | tf_op jit(solution)/shard_map/ppermute | solution.py:269
  17.3 0.8 broadcast_in_dim.12
  18.0 7.5 %all_to_all.20 = bf16[4,64,160]{2,1,0:T(8,128)(2,1)S(1)} all-to-all(bf16[4,64,160]{2,1,0:T(8,128)(2,1)S(1)} %broadcast_in_dim.12), channel_id=1, replica_groups=mesh['z'=8,'xl'=2,'c'=2,'y'=8,'xh'=2] {'xh','xl'}, dimensions={0} | all-to-all | bytes 163840 | tf_op jit(solution)/shard_map/all_to_all | solution.py:272
  25.6 0.1 copy.11
  25.7 0.8 reshape.34
  26.4 0.0 all-gather.3.cloned.1.call-update
  26.5 1.0 shard_map.104
  27.5 6.1 %all-to-all-start.1 = ((bf16[16,176,128]{2,1,0:T(8,128)(2,1)}), bf16[16,176,128]{2,1,0:T(8,128)(2,1)S(1)}, u32[]{:S(2)}, u32[]{:S(2)}) async-start(bf16[16,176,128]{2,1,0:T(8,128)(2,1)} %shard_map.104), calls=%async_computation.1 | async-start | bytes 1441792 | tf_op jit(solution)/shard_map/all_to_all | solution.py:278
  33.7 1.5 %shard_map.103 = bf16[16,2,32,640]{3,2,1,0:T(8,128)(2,1)} custom-call(bf16[128,5120]{1,0:T(8,128)(2,1)S(1)} %copy-done.1), custom_call_target="tpu_custom_call" | custom-call | bytes 2621440 | tf_op jit(solution)/shard_map/pallas_call | solution.py:52
  35.2 17.6 %all-to-all-done.1.g_ref = bf16[16,176,128]{2,1,0:T(8,128)(2,1)S(1)} async-done(((bf16[16,176,128]{2,1,0:T(8,128)(2,1)}), bf16[16,176,128]{2,1,0:T(8,128)(2,1)S(1)}, u32[]{:S(2)}, u32[]{:S(2)}) %all-to-all-start.1) | async-done | bytes 720928 | tf_op jit(solution)/shard_map/all_to_all | solution.py:278
  52.8 5.8 %all-to-all-start.2 = ((bf16[16,2,32,640]{3,2,1,0:T(8,128)(2,1)}), bf16[16,2,32,640]{3,2,1,0:T(8,128)(2,1)S(1)}, u32[]{:S(2)}, u32[]{:S(2)}) async-start(bf16[16,2,32,640]{3,2,1,0:T(8,128)(2,1)} %shard_map.103), calls=%async_computation.2 | async-start | bytes 2621440 | tf_op jit(solution)/shard_map/all_to_all | solution.py:280
  58.6 0.8 shard_map.105
  59.4 3.5 %collective-permute-start.1 = (bf16[160,128]{1,0:T(8,128)(2,1)S(1)}, bf16[160,128]{1,0:T(8,128)(2,1)S(1)}, u32[]{:S(2)}, u32[]{:S(2)}) collective-permute-start(bf16[160,128]{1,0:T(8,128)(2,1)S(1)} %get-tuple-element.17), channel_id=1, source_target_pairs={{0,1},{1,0},{2,3},{3,2},{4,5},{5,4},{6,7},{7,6},{8,9},{9,8},{10,11... | collective-permute-start | bytes 122888 | tf_op jit(solution)/shard_map/ppermute | solution.py:283
  62.9 2.7 %collective-permute-done.1 = bf16[160,128]{1,0:T(8,128)(2,1)S(1)} collective-permute-done((bf16[160,128]{1,0:T(8,128)(2,1)S(1)}, bf16[160,128]{1,0:T(8,128)(2,1)S(1)}, u32[]{:S(2)}, u32[]{:S(2)}) %collective-permute-start.1) | collective-permute-done | bytes 40992 | tf_op jit(solution)/shard_map/ppermute | solution.py:283
  65.7 23.8 %all_gather.9 = bf16[2560,128]{1,0:T(8,128)(2,1)S(1)} all-gather(bf16[320,128]{1,0:T(8,128)(2,1)S(1)} %pad_maximum_fusion), channel_id=1, replica_groups=mesh['z'=8,'xl'=2,'c'=2,'y'=8,'xh'=2] {'y'}, dimensions={0}, use_global_device_ids=true | all-gather | bytes 737280 | tf_op jit(solution)/shard_map/all_gather | solution.py:284
  89.5 9.0 %collective-permute-start.2 = (bf16[16,160,128]{2,1,0:T(8,128)(2,1)S(1)}, bf16[16,160,128]{2,1,0:T(8,128)(2,1)S(1)}, u32[]{:S(2)}, u32[]{:S(2)}) collective-permute-start(bf16[16,160,128]{2,1,0:T(8,128)(2,1)S(1)} %bitcast.21), channel_id=1, source_target_pairs={{0,16},{16,0},{1,17},{17,1},{2,18},{18,2},{3,19},{19,3},{4,20},{20... | collective-permute-start | bytes 1966088 | tf_op jit(solution)/shard_map/ppermute | solution.py:285
  98.5 0.1 pad_add_fusion.ids_ref
  98.6 3.7 %shard_map.106 = (f32[2048,128]{1,0:T(8,128)S(1)}, bf16[2048,128]{1,0:T(8,128)(2,1)S(1)}) custom-call(s32[2]{0:T(128)S(1)} %pad_add_fusion.ids_ref, bf16[16,160,128]{2,1,0:T(8,128)(2,1)S(1)} %bitcast.22, bf16[16,2,32,640]{3,2,1,0:T(8,128)(2,1)S(1)} %all-to-all-done.2.x_ref, f32[16,128]{1,0:T(8,128)S(1)} %get-tuple-element.19.route_ref), custom_call_target="tpu_custom_call" | custom-call | flops 1342177280 | bytes 4194304 | tf_op jit(solution)/shard_map/pallas_call | solution.py:166
  102.3 0.0 copy-start.6
  102.3 3.5 %shard_map.107 = bf16[2048,128]{1,0:T(8,128)(2,1)S(1)} custom-call(s32[2]{0:T(128)S(1)} %pad_add_fusion.ids_ref, bf16[16,160,128]{2,1,0:T(8,128)(2,1)S(1)} %collective-permute-done.2.w_ref, bf16[16,2,32,640]{3,2,1,0:T(8,128)(2,1)S(1)} %all-to-all-done.2.x_ref, bf16[2048,128]{1,0:T(8,128)(2,1)S(1)} %get-tuple-element.20.spread_ref, ...), custom_call_target="tpu_custom_call" | custom-call | flops 1342177280 | bytes 4194304 | tf_op jit(solution)/shard_map/pallas_call | solution.py:182
  105.8 25.8 %all_to_all.21.p_ref = bf16[16,128,128]{2,1,0:T(8,128)(2,1)S(1)} all-to-all(bf16[16,128,128]{2,1,0:T(8,128)(2,1)S(1)} %bitcast.23), channel_id=1, replica_groups=mesh['z'=8,'xl'=2,'c'=2,'y'=8,'xh'=2] {'z','xl'}, dimensions={0} | all-to-all | bytes 1048576 | tf_op jit(solution)/shard_map/all_to_all | solution.py:290
  131.7 6.4 %shard_map.108 = bf16[128,5120]{1,0:T(8,128)(2,1)} custom-call(bf16[16,128,128]{2,1,0:T(8,128)(2,1)S(1)} %all_to_all.21.p_ref, s32[1,128]{1,0:T(1,128)S(1)} %bitcast.28, f32[1,128]{1,0:T(1,128)S(1)} %bitcast.29, bf16[8,8,2,64,640]{4,3,2,1,0:T(8,128)(2,1)} %bitcast.30), custom_call_target="tpu_custom_call" | custom-call | flops 1342177280 | bytes 12582912 | tf_op jit(solution)/shard_map/pallas_call | solution.py:238
  (18 shorter events, 0.0 us)
Async XLA Ops:
  7.2 19.3 %copy-start = (bf16[1,1,5120,128]{3,2,1,0:T(8,128)(2,1)S(1)}, bf16[1,1,5120,128]{3,2,1,0:T(8,128)(2,1)}, u32[]{:S(2)}) copy-start(bf16[1,1,5120,128]{3,2,1,0:T(8,128)(2,1)} %param.8) | copy-start | bytes 3932164
  7.2 19.3 %copy-start.5 = (s32[128,1]{0,1:T(1,128)S(1)}, s32[128,1]{0,1:T(1,128)}, u32[]{:S(2)}) copy-start(s32[128,1]{0,1:T(1,128)} %param.14) | copy-start | bytes 1540
  7.2 124.5 %all-gather.3.cloned.1.call-start = ((), (), s32[]{:S(2)}) async-start(), calls=%async_computation.4 | async-start | bytes 10567680 | tf_op jit(solution)/shard_map/all_gather | solution.py:275
  8.5 18.0 %collective-permute-start = (bf16[16,160,128]{2,1,0:T(8,128)(2,1)S(1)}, bf16[16,160,128]{2,1,0:T(8,128)(2,1)S(1)}, u32[]{:S(2)}, u32[]{:S(2)}) collective-permute-start(bf16[16,160,128]{2,1,0:T(8,128)(2,1)S(1)} %dynamic-slice_bitcast_fusion), channel_id=1, source_target_pairs={{0,16},{16,0},{1,17},{17,1},{2,18},{18,2},{3,19},{19,3},{4,20},{20... | collective-permute-start | bytes 1966088 | tf_op jit(solution)/shard_map/ppermute | solution.py:269
  27.5 6.1 %copy-start.1 = (bf16[128,5120]{1,0:T(8,128)(2,1)S(1)}, bf16[128,5120]{1,0:T(8,128)(2,1)}, u32[]{:S(2)}) copy-start(bf16[128,5120]{1,0:T(8,128)(2,1)} %x_ref.1) | copy-start | bytes 3932164
  27.5 25.3 %all-to-all-start.1 = ((bf16[16,176,128]{2,1,0:T(8,128)(2,1)}), bf16[16,176,128]{2,1,0:T(8,128)(2,1)S(1)}, u32[]{:S(2)}, u32[]{:S(2)}) async-start(bf16[16,176,128]{2,1,0:T(8,128)(2,1)} %shard_map.104), calls=%async_computation.1 | async-start | bytes 1441792 | tf_op jit(solution)/shard_map/all_to_all | solution.py:278
  35.2 23.4 %copy-start.2 = (f32[1,160,128]{2,1,0:T(8,128)S(1)}, f32[1,160,128]{2,1,0:T(8,128)}, u32[]{:S(2)}) copy-start(f32[1,160,128]{2,1,0:T(8,128)} %param.9) | copy-start | bytes 245764
  35.2 23.4 %copy-start.3 = (f32[1,160,128]{2,1,0:T(8,128)S(1)}, f32[1,160,128]{2,1,0:T(8,128)}, u32[]{:S(2)}) copy-start(f32[1,160,128]{2,1,0:T(8,128)} %param.10) | copy-start | bytes 245764
  35.2 23.4 %copy-start.4 = (f32[1,160,128]{2,1,0:T(8,128)S(1)}, f32[1,160,128]{2,1,0:T(8,128)}, u32[]{:S(2)}) copy-start(f32[1,160,128]{2,1,0:T(8,128)} %param.11) | copy-start | bytes 245764
  52.8 45.8 %all-to-all-start.2 = ((bf16[16,2,32,640]{3,2,1,0:T(8,128)(2,1)}), bf16[16,2,32,640]{3,2,1,0:T(8,128)(2,1)S(1)}, u32[]{:S(2)}, u32[]{:S(2)}) async-start(bf16[16,2,32,640]{3,2,1,0:T(8,128)(2,1)} %shard_map.103), calls=%async_computation.2 | async-start | bytes 2621440 | tf_op jit(solution)/shard_map/all_to_all | solution.py:280
  59.4 6.2 %collective-permute-start.1 = (bf16[160,128]{1,0:T(8,128)(2,1)S(1)}, bf16[160,128]{1,0:T(8,128)(2,1)S(1)}, u32[]{:S(2)}, u32[]{:S(2)}) collective-permute-start(bf16[160,128]{1,0:T(8,128)(2,1)S(1)} %get-tuple-element.17), channel_id=1, source_target_pairs={{0,1},{1,0},{2,3},{3,2},{4,5},{5,4},{6,7},{7,6},{8,9},{9,8},{10,11... | collective-permute-start | bytes 122888 | tf_op jit(solution)/shard_map/ppermute | solution.py:283
  89.5 12.8 %collective-permute-start.2 = (bf16[16,160,128]{2,1,0:T(8,128)(2,1)S(1)}, bf16[16,160,128]{2,1,0:T(8,128)(2,1)S(1)}, u32[]{:S(2)}, u32[]{:S(2)}) collective-permute-start(bf16[16,160,128]{2,1,0:T(8,128)(2,1)S(1)} %bitcast.21), channel_id=1, source_target_pairs={{0,16},{16,0},{1,17},{17,1},{2,18},{18,2},{3,19},{19,3},{4,20},{20... | collective-permute-start | bytes 1966088 | tf_op jit(solution)/shard_map/ppermute | solution.py:285
  102.3 29.4 %copy-start.6 = (f32[128]{0:T(128)S(1)}, f32[128]{0:T(128)}, u32[]{:S(2)}) copy-start(f32[128]{0:T(128)} %param.15) | copy-start | bytes 1540
Sparse Core Ops, SparseCore 0:
  26.6 103.6 all-gather.2

commit v4 on v3

--- a/solution.py
+++ b/solution.py
@@ -41,10 +41,12 @@
     quarter = TOK // 4
     for k in range(o_ref.shape[0]):
         for c in range(C):
-            at = slice((k * C + c) * ROWS, (k * C + c + 1) * ROWS)
-            part = x_ref[:, at]
+            at = (k * C + c) * ROWS
+            part = x_ref[:, at : at + ROWS]
             groups = [part[q * quarter : (q + 1) * quarter] for q in range(4)]
-            o_ref[k, c] = jnp.concatenate(groups, axis=1)
+            wide = [g[:, :128] for g in groups]
+            rest = [g[:, 128:] for g in groups]
+            o_ref[k, c] = jnp.concatenate(wide + rest, axis=1)
 
 
 def pack(tokens):
@@ -118,47 +120,67 @@
     )(arrived, master, moment, second)
 
 
-def select_sums(x_ref, core, w_ref, high, x_scr, route_ref, start, store):
+def select_sums(x_ref, core, w_ref, x_scr, y_scr, place_ref, start, store):
     quarter = TOK // 4
+    lane = lax.broadcasted_iota(jnp.int32, (quarter, 128), 1)
     for s in range(GROUP):
         block = x_ref[s, core]
+        rest = block[:, 512:].astype(f32)
+        turned = [rest] + [
+            jnp.concatenate([rest[:, 128 - 32 * k :], rest[:, : 128 - 32 * k]], axis=1)
+            for k in range(1, 4)
+        ]
         for q in range(4):
-            at = s * TOK + q * quarter
-            x_scr[at : at + quarter, :] = block[:, q * ROWS : (q + 1) * ROWS]
-    step = 1024
+            at = slice(s * TOK + q * quarter, s * TOK + (q + 1) * quarter)
+            x_scr[at, :] = block[:, 128 * q : 128 * (q + 1)]
+            spread = turned[(3 - q) % 4]
+            for g in range(3):
+                spread = jnp.where((lane >= 32 * g) & (lane < 32 * (g + 1)), turned[(g - q) % 4], spread)
+            y_scr[at, :] = spread.astype(bf16)
+    half = EXPERTS // 2
+    rows_of = [jnp.concatenate([w_ref[j, :128], w_ref[j + half, :128]], axis=1) for j in range(half)]
+    rows_of += [jnp.concatenate([w_ref[j, 128:], w_ref[j + half, 128:]], axis=1) for j in range(half)]
+    weights = jnp.concatenate(rows_of, axis=0)
+    step = 512
 
     def rows(i, carry):
         at = pl.ds(pl.multiple_of(i * step, step), step)
-        kept = jnp.zeros((step, 128), f32)
-        route = route_ref[at, :].astype(f32)
-        for e in range(0, EXPERTS, 2):
-            weights = jnp.concatenate([w_ref[e], w_ref[e + 1]], axis=1)
-            both = jnp.dot(x_scr[at, :], weights, preferred_element_type=f32)
-            kept = jnp.where(route == (e + high).astype(f32), both[:, :128], kept)
-            kept = jnp.where(route == (e + 1 - high).astype(f32), both[:, 128:], kept)
+        place = place_ref[at, :]
+        group = (lax.broadcasted_iota(jnp.int32, (step, 128), 1) // 32).astype(f32).astype(bf16)
+        eight = jnp.asarray(half, bf16)
+        within = jnp.where(place >= eight, place - eight, place)
+        x = x_scr[at, :]
+        y = y_scr[at, :]
+        none = jnp.zeros((step, 128), bf16)
+        copies = [jnp.where(within == jnp.asarray(j, bf16), x, none) for j in range(half)]
+        copies += [jnp.where(within == group + jnp.asarray(4 * h, bf16), y, none) for h in range(2)]
+        both = jnp.dot(jnp.concatenate(copies, axis=1), weights, preferred_element_type=f32)
+        kept = jnp.where(place.astype(f32) >= float(half), both[:, 128:], both[:, :128])
         store(at, kept if start is None else kept + start[at, :])
         return carry
 
-    lax.fori_loop(0, GROUP * TOK // step, rows, 0)
-
-
-def first_kernel(ids_ref, w_ref, x_ref, route_ref, o_ref, spread_ref, x_scr):
-    columns = jnp.transpose(route_ref[...])
+    lax.fori_loop(0, GROUP * TOK // step, rows, 0, unroll=True)
+
+
+def first_kernel(ids_ref, w_ref, x_ref, route_ref, o_ref, place_ref, x_scr, y_scr):
+    route = route_ref[...]
+    low_bit = route - 2.0 * jnp.floor(route * 0.5)
+    columns = jnp.transpose(jnp.where(ids_ref[1] == 0, route, route + 1.0 - 2.0 * low_bit))
     for s in range(GROUP):
         wide = jnp.broadcast_to(columns[:, s : s + 1], (TOK, 128))
-        spread_ref[s * TOK : (s + 1) * TOK, :] = wide.astype(bf16)
+        place_ref[s * TOK : (s + 1) * TOK, :] = wide.astype(bf16)
 
     def store(at, value):
         o_ref[at, :] = value
 
-    select_sums(x_ref, ids_ref[0], w_ref, ids_ref[1], x_scr, spread_ref, None, store)
-
-
-def second_kernel(ids_ref, w_ref, x_ref, spread_ref, p_ref, o_ref, x_scr):
+    select_sums(x_ref, ids_ref[0], w_ref, x_scr, y_scr, place_ref, None, store)
+
+
+def second_kernel(ids_ref, w_ref, x_ref, place_ref, p_ref, o_ref, x_scr, y_scr):
     def store(at, value):
         o_ref[at, :] = value.astype(bf16)
 
-    select_sums(x_ref, 1 - ids_ref[0], w_ref, ids_ref[1], x_scr, spread_ref, p_ref, store)
+    select_sums(x_ref, 1 - ids_ref[0], w_ref, x_scr, y_scr, place_ref, p_ref, store)
 
 
 def first_sums(ids, weights, x, route):
@@ -171,23 +193,23 @@
         ),
         in_specs=[pl.BlockSpec(memory_space=pltpu.SMEM), vmem, vmem, vmem],
         out_specs=(vmem, vmem),
-        scratch_shapes=[pltpu.VMEM((GROUP * TOK, ROWS), bf16)],
+        scratch_shapes=[pltpu.VMEM((GROUP * TOK, 128), bf16)] * 2,
         compiler_params=params(20),
         cost_estimate=cost(2 * GROUP * TOK * ROWS * EXPERTS * 128, 4 * 1024 * 1024),
     )(ids, weights, x, route)
 
 
-def second_sums(ids, weights, x, spread, parts):
+def second_sums(ids, weights, x, place, parts):
     vmem = pl.BlockSpec(memory_space=pltpu.VMEM)
     return pl.pallas_call(
         second_kernel,
         out_shape=jax.ShapeDtypeStruct((GROUP * TOK, 128), bf16),
         in_specs=[pl.BlockSpec(memory_space=pltpu.SMEM)] + [vmem] * 4,
         out_specs=vmem,
-        scratch_shapes=[pltpu.VMEM((GROUP * TOK, ROWS), bf16)],
+        scratch_shapes=[pltpu.VMEM((GROUP * TOK, 128), bf16)] * 2,
         compiler_params=params(20),
         cost_estimate=cost(2 * GROUP * TOK * ROWS * EXPERTS * 128, 4 * 1024 * 1024),
-    )(ids, weights, x, spread, parts)
+    )(ids, weights, x, place, parts)
 
 
 def finish_kernel(p_ref, route_ref, prob_ref, d_ref, o_ref, w_scr, h_scr, prob_scr, sems):
@@ -218,17 +240,22 @@
 
     prob = jnp.concatenate([prob_scr[...]] * 5, axis=1)
     split = Y * UNITS
+    lane = lax.broadcasted_iota(jnp.int32, (split, 128), 1)
+
+    def beside(left, right):
+        middle = jnp.where(lane < UNITS, left[:, 256:384].astype(f32), right[:, 256:384].astype(f32))
+        return jnp.concatenate([left[:, :256], middle.astype(bf16), right[:, 384:]], axis=1)
+
     for k in range(n):
         z = step * n + k
         weights(z).wait()
-        outs = []
-        for c in range(C):
-            block = w_scr[z, :, c].reshape(split, 2 * COLS)
-            low = jnp.dot(h_scr[:, :split], block[:, :COLS], preferred_element_type=f32)
-            wide = jnp.dot(h_scr[:, split:], block[:, COLS - UNITS :], preferred_element_type=f32)
-            outs.append((low + wide[:, UNITS:]).astype(bf16))
-        even, odd = outs
-        blocks = [even[:, :ROWS], odd[:, :ROWS], even[:, ROWS:], odd[:, ROWS:]]
+        even = w_scr[z, :, 0].reshape(split, 2 * COLS)
+        odd = w_scr[z, :, 1].reshape(split, 2 * COLS)
+        low = jnp.dot(h_scr[:, :split], beside(even, odd), preferred_element_type=f32)
+        high = jnp.dot(h_scr[:, split:], beside(odd, even), preferred_element_type=f32)
+        total = low + jnp.concatenate([high[:, COLS:], high[:, :COLS]], axis=1)
+        total = total.astype(bf16)
+        blocks = [total[:, i * ROWS : (i + 1) * ROWS] for i in (0, 2, 1, 3)]
         whole = jnp.concatenate(blocks, axis=1).astype(f32)
         o_ref[:, k * 2 * COLS : (k + 1) * 2 * COLS] = (prob * whole).astype(bf16)
 
@@ -271,6 +298,7 @@
     down = jnp.broadcast_to(down_weight[0].T[None], (XH * XL, UNITS, ROWS))
     four = lax.all_to_all(down, ("xh", "xl"), 0, 0, tiled=True)
     pair = jnp.transpose(four, (1, 0, 2)).reshape(UNITS, 2 * COLS)
+    pair = jnp.where(core == 0, pair, jnp.concatenate([pair[:, COLS:], pair[:, :COLS]], 1))
     pair, received = lax.optimization_barrier((pair, received))
     down_all = lax.all_gather(pair, ("z", "y", "c"), axis=0, tiled=False)
     down_all = down_all.reshape(Z, Y, C, UNITS, 2 * COLS)
@@ -285,8 +313,8 @@
     other = lax.ppermute(own, "c", SWAP)
 
     ids = jnp.stack([core, high]).astype(jnp.int32)
-    parts, spread = first_sums(ids, own, columns, route_all)
-    parts = second_sums(ids, other, columns, spread, parts)
+    parts, place = first_sums(ids, own, columns, route_all)
+    parts = second_sums(ids, other, columns, place, parts)
     parts = lax.all_to_all(parts.reshape(GROUP, TOK, 128), group, 0, 0, tiled=True)
     mixed = finish(parts, routes.reshape(1, TOK), probs.reshape(1, TOK), down_all)
     return new_master[None], new_moment[None], mixed

time: 145 us -> 146 us (level)
  waiting for transfers between devices: 20.4 us -> 25.2 us
  blocking collectives: 57.2 us -> 52.7 us
  Pallas kernels: 16.9 us -> 14.1 us
  starting transfers between devices: 33.3 us -> 35.6 us
    all_to_all x1 -> x0, blocking collectives: 7.51 us -> none  [shards(): four = lax.all_to_all(down, ('xh', 'xl'), 0, 0, tiled=True)]
    all_to_all x0 -> x1, waiting for transfers between devices: none -> 5.04 us  [shards(): four = lax.all_to_all(down, ('xh', 'xl'), 0, 0, tiled=True)]
    all_to_all x0 -> x1, starting transfers between devices: none -> 3.33 us  [shards(): four = lax.all_to_all(down, ('xh', 'xl'), 0, 0, tiled=True)]
    all_to_all x1, blocking collectives: 25.8 us -> 28.5 us  [shards(): lax.all_to_all(parts.reshape(GROUP, TOK, 128), group, 0, 0, tiled=True)]
  transfers between devices with their start and end apart: 6 -> 7, of which waited for: 2 -> 3; matrix products, arithmetic and copies ran while one was open for 1% -> 1% of each run, Pallas kernels for 7% -> 6%
where the time goes in v4:
time: 146 us; the launch traced here: 145 us
  blocking collectives  52.7 us (36%)
  starting transfers between devices  35.6 us (24%)
  waiting for transfers between devices  25.2 us (17%)
  between operations  14.2 us (10%)
  Pallas kernels  14.1 us (10%)
  local copies, waits for them, and re-layouts  2.26 us (2%)
    all_to_all x1, blocking collectives, shards(): lax.all_to_all(parts.reshape(GROUP, TOK, 128), group, 0, 0, tiled=True)  28.5 us
    all_gather x1, blocking collectives, shards(): lax.all_gather(pair_short, 'y', axis=0, tiled=True)  24.2 us
    all_to_all x1, waiting for transfers between devices, shards(): arrived = lax.all_to_all(chunk, group, 0, 0, tiled=True)  17.4 us
    ppermute x1, starting transfers between devices, shards(): received = lax.ppermute(sent, 'c', SWAP)  8.79 us
    ppermute x1, starting transfers between devices, shards(): other = lax.ppermute(own, 'c', SWAP)  8.71 us
    all_to_all x1, starting transfers between devices, shards(): columns = lax.all_to_all(packed, group, 0, 0, tiled=True)  5.8 us
    pallas_call x1, Pallas kernels, finish(): pl.pallas_call(finish_kernel, out_shape=jax.ShapeDtypeStruct((TOK, D), bf...  5.77 us
    all_to_all x1, starting transfers between devices, shards(): arrived = lax.all_to_all(chunk, group, 0, 0, tiled=True)  5.42 us
  transfers between devices with their start and end apart: 7, of which 3 were waited for; matrix products, arithmetic and copies ran while one was open for 1% of the time, Pallas kernels for 6%

profile of v4, /device:TPU:1, one launch (start us, length us, event | category | flops | bytes accessed | tf_op | source)
XLA Modules:
  0.0 145.0 jit_solution(12988909766762760899)
XLA Ops:
  7.2 1.2 dynamic-slice_bitcast_fusion
  8.4 8.8 %collective-permute-start = (bf16[16,160,128]{2,1,0:T(8,128)(2,1)S(1)}, bf16[16,160,128]{2,1,0:T(8,128)(2,1)S(1)}, u32[]{:S(2)}, u32[]{:S(2)}) collective-permute-start(bf16[16,160,128]{2,1,0:T(8,128)(2,1)S(1)} %dynamic-slice_bitcast_fusion), channel_id=1, source_target_pairs={{0,16},{16,0},{1,17},{17,1},{2,18},{18,2},{3,19},{19,3},{4,20},{20... | collective-permute-start | bytes 1966088 | tf_op jit(solution)/shard_map/ppermute | solution.py:296
  17.2 0.7 broadcast_in_dim.12
  17.9 3.3 %all-to-all-start = ((bf16[4,64,160]{2,1,0:T(8,128)(2,1)}), bf16[4,64,160]{2,1,0:T(8,128)(2,1)S(1)}, u32[]{:S(2)}, u32[]{:S(2)}) async-start(bf16[4,64,160]{2,1,0:T(8,128)(2,1)} %broadcast_in_dim.12), calls=%async_computation | async-start | bytes 262144 | tf_op jit(solution)/shard_map/all_to_all | solution.py:299
  21.3 5.0 %all-to-all-done = bf16[4,64,160]{2,1,0:T(8,128)(2,1)S(1)} async-done(((bf16[4,64,160]{2,1,0:T(8,128)(2,1)}), bf16[4,64,160]{2,1,0:T(8,128)(2,1)S(1)}, u32[]{:S(2)}, u32[]{:S(2)}) %all-to-all-start) | async-done | bytes 81952 | tf_op jit(solution)/shard_map/all_to_all | solution.py:299
  26.3 0.1 copy.11
  26.4 0.1 reshape.34
  26.6 0.1 fusion
  26.7 0.7 maximum_select_fusion
  27.5 1.0 shard_map.104
  28.5 5.4 %all-to-all-start.1 = ((bf16[16,176,128]{2,1,0:T(8,128)(2,1)}), bf16[16,176,128]{2,1,0:T(8,128)(2,1)S(1)}, u32[]{:S(2)}, u32[]{:S(2)}) async-start(bf16[16,176,128]{2,1,0:T(8,128)(2,1)} %shard_map.104), calls=%async_computation.1 | async-start | bytes 1441792 | tf_op jit(solution)/shard_map/all_to_all | solution.py:306
  33.9 1.7 %shard_map.103 = bf16[16,2,32,640]{3,2,1,0:T(8,128)(2,1)} custom-call(bf16[128,5120]{1,0:T(8,128)(2,1)S(1)} %copy-done.1), custom_call_target="tpu_custom_call" | custom-call | bytes 2621440 | tf_op jit(solution)/shard_map/pallas_call | solution.py:54
  35.6 17.4 %all-to-all-done.1.g_ref = bf16[16,176,128]{2,1,0:T(8,128)(2,1)S(1)} async-done(((bf16[16,176,128]{2,1,0:T(8,128)(2,1)}), bf16[16,176,128]{2,1,0:T(8,128)(2,1)S(1)}, u32[]{:S(2)}, u32[]{:S(2)}) %all-to-all-start.1) | async-done | bytes 720928 | tf_op jit(solution)/shard_map/all_to_all | solution.py:306
  53.1 5.8 %all-to-all-start.2 = ((bf16[16,2,32,640]{3,2,1,0:T(8,128)(2,1)}), bf16[16,2,32,640]{3,2,1,0:T(8,128)(2,1)S(1)}, u32[]{:S(2)}, u32[]{:S(2)}) async-start(bf16[16,2,32,640]{3,2,1,0:T(8,128)(2,1)} %shard_map.103), calls=%async_computation.2 | async-start | bytes 2621440 | tf_op jit(solution)/shard_map/all_to_all | solution.py:308
  58.9 0.8 shard_map.105
  59.7 3.5 %collective-permute-start.1 = (bf16[160,128]{1,0:T(8,128)(2,1)S(1)}, bf16[160,128]{1,0:T(8,128)(2,1)S(1)}, u32[]{:S(2)}, u32[]{:S(2)}) collective-permute-start(bf16[160,128]{1,0:T(8,128)(2,1)S(1)} %get-tuple-element.17), channel_id=1, source_target_pairs={{0,1},{1,0},{2,3},{3,2},{4,5},{5,4},{6,7},{7,6},{8,9},{9,8},{10,11... | collective-permute-start | bytes 122888 | tf_op jit(solution)/shard_map/ppermute | solution.py:311
  63.2 2.7 %collective-permute-done.1 = bf16[160,128]{1,0:T(8,128)(2,1)S(1)} collective-permute-done((bf16[160,128]{1,0:T(8,128)(2,1)S(1)}, bf16[160,128]{1,0:T(8,128)(2,1)S(1)}, u32[]{:S(2)}, u32[]{:S(2)}) %collective-permute-start.1) | collective-permute-done | bytes 40992 | tf_op jit(solution)/shard_map/ppermute | solution.py:311
  66.0 24.2 %all_gather.9 = bf16[2560,128]{1,0:T(8,128)(2,1)S(1)} all-gather(bf16[320,128]{1,0:T(8,128)(2,1)S(1)} %pad_maximum_fusion), channel_id=1, replica_groups=mesh['z'=8,'xl'=2,'c'=2,'y'=8,'xh'=2] {'y'}, dimensions={0}, use_global_device_ids=true | all-gather | bytes 737280 | tf_op jit(solution)/shard_map/all_gather | solution.py:312
  90.1 8.7 %collective-permute-start.2 = (bf16[16,160,128]{2,1,0:T(8,128)(2,1)S(1)}, bf16[16,160,128]{2,1,0:T(8,128)(2,1)S(1)}, u32[]{:S(2)}, u32[]{:S(2)}) collective-permute-start(bf16[16,160,128]{2,1,0:T(8,128)(2,1)S(1)} %bitcast.21), channel_id=1, source_target_pairs={{0,16},{16,0},{1,17},{17,1},{2,18},{18,2},{3,19},{19,3},{4,20},{20... | collective-permute-start | bytes 1966088 | tf_op jit(solution)/shard_map/ppermute | solution.py:313
  98.9 0.1 pad_add_fusion.ids_ref
  98.9 2.5 %shard_map.106 = (f32[2048,128]{1,0:T(8,128)S(1)}, bf16[2048,128]{1,0:T(8,128)(2,1)S(1)}) custom-call(s32[2]{0:T(128)S(1)} %pad_add_fusion.ids_ref, bf16[16,160,128]{2,1,0:T(8,128)(2,1)S(1)} %bitcast.22, bf16[16,2,32,640]{3,2,1,0:T(8,128)(2,1)S(1)} %all-to-all-done.2.x_ref, f32[16,128]{1,0:T(8,128)S(1)} %get-tuple-element.19.route_ref), custom_call_target="tpu_custom_call" | custom-call | flops 1342177280 | bytes 4194304 | tf_op jit(solution)/shard_map/pallas_call | solution.py:188
  101.5 2.4 %shard_map.107 = bf16[2048,128]{1,0:T(8,128)(2,1)S(1)} custom-call(s32[2]{0:T(128)S(1)} %pad_add_fusion.ids_ref, bf16[16,160,128]{2,1,0:T(8,128)(2,1)S(1)} %collective-permute-done.2.w_ref, bf16[16,2,32,640]{3,2,1,0:T(8,128)(2,1)S(1)} %all-to-all-done.2.x_ref, bf16[2048,128]{1,0:T(8,128)(2,1)S(1)} %get-tuple-element.20.place_ref, ...), custom_call_target="tpu_custom_call" | custom-call | flops 1342177280 | bytes 4194304 | tf_op jit(solution)/shard_map/pallas_call | solution.py:204
  103.8 28.5 %all_to_all.20.p_ref = bf16[16,128,128]{2,1,0:T(8,128)(2,1)S(1)} all-to-all(bf16[16,128,128]{2,1,0:T(8,128)(2,1)S(1)} %bitcast.23), channel_id=1, replica_groups=mesh['z'=8,'xl'=2,'c'=2,'y'=8,'xh'=2] {'z','xl'}, dimensions={0} | all-to-all | bytes 1048576 | tf_op jit(solution)/shard_map/all_to_all | solution.py:318
  132.3 5.8 %shard_map.108 = bf16[128,5120]{1,0:T(8,128)(2,1)} custom-call(bf16[16,128,128]{2,1,0:T(8,128)(2,1)S(1)} %all_to_all.20.p_ref, s32[1,128]{1,0:T(1,128)S(1)} %bitcast.28, f32[1,128]{1,0:T(1,128)S(1)} %bitcast.29, bf16[8,8,2,64,640]{4,3,2,1,0:T(8,128)(2,1)} %bitcast.30), custom_call_target="tpu_custom_call" | custom-call | flops 1342177280 | bytes 12582912 | tf_op jit(solution)/shard_map/pallas_call | solution.py:265
  (23 shorter events, 0.1 us)
Async XLA Ops:
  7.2 10.1 %copy-start.7 = (bf16[1,160,64]{1,2,0:T(8,128)(2,1)S(1)}, bf16[1,160,64]{1,2,0:T(8,128)(2,1)}, u32[]{:S(2)}) copy-start(bf16[1,160,64]{1,2,0:T(8,128)(2,1)} %param.12) | copy-start | bytes 61444
  7.2 20.3 %copy-start = (bf16[1,1,5120,128]{3,2,1,0:T(8,128)(2,1)S(1)}, bf16[1,1,5120,128]{3,2,1,0:T(8,128)(2,1)}, u32[]{:S(2)}) copy-start(bf16[1,1,5120,128]{3,2,1,0:T(8,128)(2,1)} %param.8) | copy-start | bytes 3932164
  7.2 20.3 %copy-start.5 = (s32[128,1]{0,1:T(1,128)S(1)}, s32[128,1]{0,1:T(1,128)}, u32[]{:S(2)}) copy-start(s32[128,1]{0,1:T(1,128)} %param.14) | copy-start | bytes 1540
  8.4 19.0 %collective-permute-start = (bf16[16,160,128]{2,1,0:T(8,128)(2,1)S(1)}, bf16[16,160,128]{2,1,0:T(8,128)(2,1)S(1)}, u32[]{:S(2)}, u32[]{:S(2)}) collective-permute-start(bf16[16,160,128]{2,1,0:T(8,128)(2,1)S(1)} %dynamic-slice_bitcast_fusion), channel_id=1, source_target_pairs={{0,16},{16,0},{1,17},{17,1},{2,18},{18,2},{3,19},{19,3},{4,20},{20... | collective-permute-start | bytes 1966088 | tf_op jit(solution)/shard_map/ppermute | solution.py:296
  17.9 8.4 %all-to-all-start = ((bf16[4,64,160]{2,1,0:T(8,128)(2,1)}), bf16[4,64,160]{2,1,0:T(8,128)(2,1)S(1)}, u32[]{:S(2)}, u32[]{:S(2)}) async-start(bf16[4,64,160]{2,1,0:T(8,128)(2,1)} %broadcast_in_dim.12), calls=%async_computation | async-start | bytes 262144 | tf_op jit(solution)/shard_map/all_to_all | solution.py:299
  21.2 111.1 %all-gather.3.cloned.1.call-start = ((), (), s32[]{:S(2)}) async-start(), calls=%async_computation.4 | async-start | bytes 10567680 | tf_op jit(solution)/shard_map/all_gather | solution.py:303
  28.5 5.4 %copy-start.1 = (bf16[128,5120]{1,0:T(8,128)(2,1)S(1)}, bf16[128,5120]{1,0:T(8,128)(2,1)}, u32[]{:S(2)}) copy-start(bf16[128,5120]{1,0:T(8,128)(2,1)} %x_ref.1) | copy-start | bytes 3932164
  28.5 24.6 %all-to-all-start.1 = ((bf16[16,176,128]{2,1,0:T(8,128)(2,1)}), bf16[16,176,128]{2,1,0:T(8,128)(2,1)S(1)}, u32[]{:S(2)}, u32[]{:S(2)}) async-start(bf16[16,176,128]{2,1,0:T(8,128)(2,1)} %shard_map.104), calls=%async_computation.1 | async-start | bytes 1441792 | tf_op jit(solution)/shard_map/all_to_all | solution.py:306
  35.6 23.3 %copy-start.2 = (f32[1,160,128]{2,1,0:T(8,128)S(1)}, f32[1,160,128]{2,1,0:T(8,128)}, u32[]{:S(2)}) copy-start(f32[1,160,128]{2,1,0:T(8,128)} %param.9) | copy-start | bytes 245764
  35.6 23.3 %copy-start.3 = (f32[1,160,128]{2,1,0:T(8,128)S(1)}, f32[1,160,128]{2,1,0:T(8,128)}, u32[]{:S(2)}) copy-start(f32[1,160,128]{2,1,0:T(8,128)} %param.10) | copy-start | bytes 245764
  35.6 23.3 %copy-start.4 = (f32[1,160,128]{2,1,0:T(8,128)S(1)}, f32[1,160,128]{2,1,0:T(8,128)}, u32[]{:S(2)}) copy-start(f32[1,160,128]{2,1,0:T(8,128)} %param.11) | copy-start | bytes 245764
  53.1 45.9 %all-to-all-start.2 = ((bf16[16,2,32,640]{3,2,1,0:T(8,128)(2,1)}), bf16[16,2,32,640]{3,2,1,0:T(8,128)(2,1)S(1)}, u32[]{:S(2)}, u32[]{:S(2)}) async-start(bf16[16,2,32,640]{3,2,1,0:T(8,128)(2,1)} %shard_map.103), calls=%async_computation.2 | async-start | bytes 2621440 | tf_op jit(solution)/shard_map/all_to_all | solution.py:308
  59.7 6.2 %collective-permute-start.1 = (bf16[160,128]{1,0:T(8,128)(2,1)S(1)}, bf16[160,128]{1,0:T(8,128)(2,1)S(1)}, u32[]{:S(2)}, u32[]{:S(2)}) collective-permute-start(bf16[160,128]{1,0:T(8,128)(2,1)S(1)} %get-tuple-element.17), channel_id=1, source_target_pairs={{0,1},{1,0},{2,3},{3,2},{4,5},{5,4},{6,7},{7,6},{8,9},{9,8},{10,11... | collective-permute-start | bytes 122888 | tf_op jit(solution)/shard_map/ppermute | solution.py:311
  90.1 11.3 %collective-permute-start.2 = (bf16[16,160,128]{2,1,0:T(8,128)(2,1)S(1)}, bf16[16,160,128]{2,1,0:T(8,128)(2,1)S(1)}, u32[]{:S(2)}, u32[]{:S(2)}) collective-permute-start(bf16[16,160,128]{2,1,0:T(8,128)(2,1)S(1)} %bitcast.21), channel_id=1, source_target_pairs={{0,16},{16,0},{1,17},{17,1},{2,18},{18,2},{3,19},{19,3},{4,20},{20... | collective-permute-start | bytes 1966088 | tf_op jit(solution)/shard_map/ppermute | solution.py:313
  101.4 30.9 %copy-start.6 = (f32[128]{0:T(128)S(1)}, f32[128]{0:T(128)}, u32[]{:S(2)}) copy-start(f32[128]{0:T(128)} %param.15) | copy-start | bytes 1540
Sparse Core Ops, SparseCore 0:
  27.6 104.2 all-gather.2

commit v5 on v4

--- a/solution.py
+++ b/solution.py
@@ -212,7 +212,36 @@
     )(ids, weights, x, place, parts)
 
 
-def finish_kernel(p_ref, route_ref, prob_ref, d_ref, o_ref, w_scr, h_scr, prob_scr, sems):
+def hidden_kernel(p_ref, route_ref, prob_ref, h_ref, wide_ref):
+    total = p_ref[0].astype(f32)
+    for i in range(1, GROUP):
+        total = total + p_ref[i].astype(f32)
+    gate = total[:, :UNITS]
+    up = total[:, UNITS:]
+    hidden = gate * jax.nn.sigmoid(gate) * up
+    rows = [jnp.broadcast_to(r, (4, TOK)) for r in (route_ref[...].astype(f32), prob_ref[...])]
+    columns = jnp.transpose(jnp.concatenate(rows, axis=0))
+    route = jnp.broadcast_to(columns[:, 0:1], (TOK, UNITS))
+    wide_ref[...] = jnp.broadcast_to(columns[:, 4:5], (TOK, 128))
+    for j in range(XH):
+        for y in range(Y):
+            at = (j * Y + y) * UNITS
+            h_ref[:, at : at + UNITS] = jnp.where(route == 2.0 * y + j, hidden, 0.0).astype(bf16)
+
+
+def hidden_units(parts, route_row, prob_row):
+    return pl.pallas_call(
+        hidden_kernel,
+        out_shape=(
+            jax.ShapeDtypeStruct((TOK, EXPERTS * UNITS), bf16),
+            jax.ShapeDtypeStruct((TOK, 128), f32),
+        ),
+        compiler_params=params(6),
+        cost_estimate=cost(0, GROUP * TOK * 256),
+    )(parts, route_row, prob_row)
+
+
+def finish_kernel(h_ref, prob_ref, d_ref, o_ref, w_scr, sems):
     step = pl.program_id(0)
     n = Z // pl.num_programs(0)
 
@@ -223,22 +252,8 @@
     def _():
         for z in range(Z):
             weights(z).start()
-        total = p_ref[0].astype(f32)
-        for i in range(1, GROUP):
-            total = total + p_ref[i].astype(f32)
-        gate = total[:, :UNITS]
-        up = total[:, UNITS:]
-        hidden = gate * jax.nn.sigmoid(gate) * up
-        rows = [jnp.broadcast_to(r, (4, TOK)) for r in (route_ref[...].astype(f32), prob_ref[...])]
-        columns = jnp.transpose(jnp.concatenate(rows, axis=0))
-        route = jnp.broadcast_to(columns[:, 0:1], (TOK, UNITS))
-        prob_scr[...] = jnp.broadcast_to(columns[:, 4:5], (TOK, 128))
-        for j in range(XH):
-            for y in range(Y):
-                at = (j * Y + y) * UNITS
-                h_scr[:, at : at + UNITS] = jnp.where(route == 2.0 * y + j, hidden, 0.0).astype(bf16)
-
-    prob = jnp.concatenate([prob_scr[...]] * 5, axis=1)
+
+    prob = jnp.concatenate([prob_ref[...]] * 5, axis=1)
     split = Y * UNITS
     lane = lax.broadcasted_iota(jnp.int32, (split, 128), 1)
 
@@ -251,8 +266,8 @@
         weights(z).wait()
         even = w_scr[z, :, 0].reshape(split, 2 * COLS)
         odd = w_scr[z, :, 1].reshape(split, 2 * COLS)
-        low = jnp.dot(h_scr[:, :split], beside(even, odd), preferred_element_type=f32)
-        high = jnp.dot(h_scr[:, split:], beside(odd, even), preferred_element_type=f32)
+        low = jnp.dot(h_ref[:, :split], beside(even, odd), preferred_element_type=f32)
+        high = jnp.dot(h_ref[:, split:], beside(odd, even), preferred_element_type=f32)
         total = low + jnp.concatenate([high[:, COLS:], high[:, :COLS]], axis=1)
         total = total.astype(bf16)
         blocks = [total[:, i * ROWS : (i + 1) * ROWS] for i in (0, 2, 1, 3)]
@@ -260,28 +275,25 @@
         o_ref[:, k * 2 * COLS : (k + 1) * 2 * COLS] = (prob * whole).astype(bf16)
 
 
-def finish(parts, route_row, prob_row, down):
+def finish(hidden, prob, down):
     steps = 4
     return pl.pallas_call(
         finish_kernel,
         out_shape=jax.ShapeDtypeStruct((TOK, D), bf16),
         grid=(steps,),
         in_specs=[
-            pl.BlockSpec((GROUP, TOK, 128), lambda i: (0, 0, 0)),
-            pl.BlockSpec((1, TOK), lambda i: (0, 0)),
-            pl.BlockSpec((1, TOK), lambda i: (0, 0)),
+            pl.BlockSpec((TOK, EXPERTS * UNITS), lambda i: (0, 0)),
+            pl.BlockSpec((TOK, 128), lambda i: (0, 0)),
             pl.BlockSpec(memory_space=pl.ANY),
         ],
         out_specs=pl.BlockSpec((TOK, D // steps), lambda i: (0, i)),
         scratch_shapes=[
             pltpu.VMEM((Z, Y, C, UNITS, 2 * COLS), bf16),
-            pltpu.VMEM((TOK, EXPERTS * UNITS), bf16),
-            pltpu.VMEM((TOK, 128), f32),
             pltpu.SemaphoreType.DMA((Z,)),
         ],
         compiler_params=params(52),
         cost_estimate=cost(2 * TOK * EXPERTS * UNITS * D, 12 * 1024 * 1024),
-    )(parts, route_row, prob_row, down)
+    )(hidden, prob, down)
 
 
 def shards(grad_parts, master, moment, second, down_weight, tokens, routes, probs):
@@ -316,7 +328,8 @@
     parts, place = first_sums(ids, own, columns, route_all)
     parts = second_sums(ids, other, columns, place, parts)
     parts = lax.all_to_all(parts.reshape(GROUP, TOK, 128), group, 0, 0, tiled=True)
-    mixed = finish(parts, routes.reshape(1, TOK), probs.reshape(1, TOK), down_all)
+    hidden, prob = hidden_units(parts, routes.reshape(1, TOK), probs.reshape(1, TOK))
+    mixed = finish(hidden, prob, down_all)
     return new_master[None], new_moment[None], mixed
 
 

time: 146 us -> 147 us (level)
  no operation moved by 1% of the time
where the time goes in v5:
time: 147 us; the launch traced here: 146 us
  blocking collectives  53.5 us (36%)
  starting transfers between devices  35.6 us (24%)
  waiting for transfers between devices  25.2 us (17%)
  Pallas kernels  14.5 us (10%)
  between operations  14.2 us (10%)
  local copies, waits for them, and re-layouts  2.26 us (2%)
    all_to_all x1, blocking collectives, shards(): lax.all_to_all(parts.reshape(GROUP, TOK, 128), group, 0, 0, tiled=True)  29.5 us
    all_gather x1, blocking collectives, shards(): lax.all_gather(pair_short, 'y', axis=0, tiled=True)  24.1 us
    all_to_all x1, waiting for transfers between devices, shards(): arrived = lax.all_to_all(chunk, group, 0, 0, tiled=True)  17.4 us
    ppermute x1, starting transfers between devices, shards(): received = lax.ppermute(sent, 'c', SWAP)  8.79 us
    ppermute x1, starting transfers between devices, shards(): other = lax.ppermute(own, 'c', SWAP)  8.72 us
    all_to_all x1, starting transfers between devices, shards(): columns = lax.all_to_all(packed, group, 0, 0, tiled=True)  5.8 us
    pallas_call x1, Pallas kernels, finish(): pl.pallas_call(finish_kernel, out_shape=jax.ShapeDtypeStruct((TOK, D), bf...  5.78 us
    all_to_all x1, starting transfers between devices, shards(): arrived = lax.all_to_all(chunk, group, 0, 0, tiled=True)  5.42 us
  transfers between devices with their start and end apart: 7, of which 3 were waited for; matrix products, arithmetic and copies ran while one was open for 1% of the time, Pallas kernels for 6%

profile of v5, /device:TPU:1, one launch (start us, length us, event | category | flops | bytes accessed | tf_op | source)
XLA Modules:
  0.0 146.2 jit_solution(9406210627401119880)
XLA Ops:
  7.2 1.2 dynamic-slice_bitcast_fusion
  8.4 8.8 %collective-permute-start = (bf16[16,160,128]{2,1,0:T(8,128)(2,1)S(1)}, bf16[16,160,128]{2,1,0:T(8,128)(2,1)S(1)}, u32[]{:S(2)}, u32[]{:S(2)}) collective-permute-start(bf16[16,160,128]{2,1,0:T(8,128)(2,1)S(1)} %dynamic-slice_bitcast_fusion), channel_id=1, source_target_pairs={{0,16},{16,0},{1,17},{17,1},{2,18},{18,2},{3,19},{19,3},{4,20},{20... | collective-permute-start | bytes 1966088 | tf_op jit(solution)/shard_map/ppermute | solution.py:308
  17.2 0.7 broadcast_in_dim.12
  17.9 3.3 %all-to-all-start = ((bf16[4,64,160]{2,1,0:T(8,128)(2,1)}), bf16[4,64,160]{2,1,0:T(8,128)(2,1)S(1)}, u32[]{:S(2)}, u32[]{:S(2)}) async-start(bf16[4,64,160]{2,1,0:T(8,128)(2,1)} %broadcast_in_dim.12), calls=%async_computation | async-start | bytes 262144 | tf_op jit(solution)/shard_map/all_to_all | solution.py:311
  21.3 5.0 %all-to-all-done = bf16[4,64,160]{2,1,0:T(8,128)(2,1)S(1)} async-done(((bf16[4,64,160]{2,1,0:T(8,128)(2,1)}), bf16[4,64,160]{2,1,0:T(8,128)(2,1)S(1)}, u32[]{:S(2)}, u32[]{:S(2)}) %all-to-all-start) | async-done | bytes 81952 | tf_op jit(solution)/shard_map/all_to_all | solution.py:311
  26.3 0.1 copy.11
  26.4 0.1 reshape.34
  26.6 0.1 fusion
  26.7 0.7 maximum_select_fusion
  27.4 1.0 shard_map.104
  28.5 5.4 %all-to-all-start.1 = ((bf16[16,176,128]{2,1,0:T(8,128)(2,1)}), bf16[16,176,128]{2,1,0:T(8,128)(2,1)S(1)}, u32[]{:S(2)}, u32[]{:S(2)}) async-start(bf16[16,176,128]{2,1,0:T(8,128)(2,1)} %shard_map.104), calls=%async_computation.1 | async-start | bytes 1441792 | tf_op jit(solution)/shard_map/all_to_all | solution.py:318
  33.9 1.7 %shard_map.103 = bf16[16,2,32,640]{3,2,1,0:T(8,128)(2,1)} custom-call(bf16[128,5120]{1,0:T(8,128)(2,1)S(1)} %copy-done.1), custom_call_target="tpu_custom_call" | custom-call | bytes 2621440 | tf_op jit(solution)/shard_map/pallas_call | solution.py:54
  35.6 17.4 %all-to-all-done.1.g_ref = bf16[16,176,128]{2,1,0:T(8,128)(2,1)S(1)} async-done(((bf16[16,176,128]{2,1,0:T(8,128)(2,1)}), bf16[16,176,128]{2,1,0:T(8,128)(2,1)S(1)}, u32[]{:S(2)}, u32[]{:S(2)}) %all-to-all-start.1) | async-done | bytes 720928 | tf_op jit(solution)/shard_map/all_to_all | solution.py:318
  53.0 5.8 %all-to-all-start.2 = ((bf16[16,2,32,640]{3,2,1,0:T(8,128)(2,1)}), bf16[16,2,32,640]{3,2,1,0:T(8,128)(2,1)S(1)}, u32[]{:S(2)}, u32[]{:S(2)}) async-start(bf16[16,2,32,640]{3,2,1,0:T(8,128)(2,1)} %shard_map.103), calls=%async_computation.2 | async-start | bytes 2621440 | tf_op jit(solution)/shard_map/all_to_all | solution.py:320
  58.9 0.8 shard_map.105
  59.7 3.5 %collective-permute-start.1 = (bf16[160,128]{1,0:T(8,128)(2,1)S(1)}, bf16[160,128]{1,0:T(8,128)(2,1)S(1)}, u32[]{:S(2)}, u32[]{:S(2)}) collective-permute-start(bf16[160,128]{1,0:T(8,128)(2,1)S(1)} %get-tuple-element.19), channel_id=1, source_target_pairs={{0,1},{1,0},{2,3},{3,2},{4,5},{5,4},{6,7},{7,6},{8,9},{9,8},{10,11... | collective-permute-start | bytes 122888 | tf_op jit(solution)/shard_map/ppermute | solution.py:323
  63.2 2.7 %collective-permute-done.1 = bf16[160,128]{1,0:T(8,128)(2,1)S(1)} collective-permute-done((bf16[160,128]{1,0:T(8,128)(2,1)S(1)}, bf16[160,128]{1,0:T(8,128)(2,1)S(1)}, u32[]{:S(2)}, u32[]{:S(2)}) %collective-permute-start.1) | collective-permute-done | bytes 40992 | tf_op jit(solution)/shard_map/ppermute | solution.py:323
  65.9 24.1 %all_gather.9 = bf16[2560,128]{1,0:T(8,128)(2,1)S(1)} all-gather(bf16[320,128]{1,0:T(8,128)(2,1)S(1)} %pad_maximum_fusion), channel_id=1, replica_groups=mesh['z'=8,'xl'=2,'c'=2,'y'=8,'xh'=2] {'y'}, dimensions={0}, use_global_device_ids=true | all-gather | bytes 737280 | tf_op jit(solution)/shard_map/all_gather | solution.py:324
  90.0 8.7 %collective-permute-start.2 = (bf16[16,160,128]{2,1,0:T(8,128)(2,1)S(1)}, bf16[16,160,128]{2,1,0:T(8,128)(2,1)S(1)}, u32[]{:S(2)}, u32[]{:S(2)}) collective-permute-start(bf16[16,160,128]{2,1,0:T(8,128)(2,1)S(1)} %bitcast.21), channel_id=1, source_target_pairs={{0,16},{16,0},{1,17},{17,1},{2,18},{18,2},{3,19},{19,3},{4,20},{20... | collective-permute-start | bytes 1966088 | tf_op jit(solution)/shard_map/ppermute | solution.py:325
  98.8 2.5 %shard_map.106 = (f32[2048,128]{1,0:T(8,128)S(1)}, bf16[2048,128]{1,0:T(8,128)(2,1)S(1)}) custom-call(s32[2]{0:T(128)S(1)} %pad_add_fusion.ids_ref, bf16[16,160,128]{2,1,0:T(8,128)(2,1)S(1)} %bitcast.22, bf16[16,2,32,640]{3,2,1,0:T(8,128)(2,1)S(1)} %all-to-all-done.2.x_ref, f32[16,128]{1,0:T(8,128)S(1)} %get-tuple-element.21.route_ref), custom_call_target="tpu_custom_call" | custom-call | flops 1342177280 | bytes 4194304 | tf_op jit(solution)/shard_map/pallas_call | solution.py:188
  101.3 2.4 %shard_map.107 = bf16[2048,128]{1,0:T(8,128)(2,1)S(1)} custom-call(s32[2]{0:T(128)S(1)} %pad_add_fusion.ids_ref, bf16[16,160,128]{2,1,0:T(8,128)(2,1)S(1)} %collective-permute-done.2.w_ref, bf16[16,2,32,640]{3,2,1,0:T(8,128)(2,1)S(1)} %all-to-all-done.2.x_ref, bf16[2048,128]{1,0:T(8,128)(2,1)S(1)} %get-tuple-element.22.place_ref, ...), custom_call_target="tpu_custom_call" | custom-call | flops 1342177280 | bytes 4194304 | tf_op jit(solution)/shard_map/pallas_call | solution.py:204
  103.7 29.5 %all_to_all.20.p_ref = bf16[16,128,128]{2,1,0:T(8,128)(2,1)S(1)} all-to-all(bf16[16,128,128]{2,1,0:T(8,128)(2,1)S(1)} %bitcast.23), channel_id=1, replica_groups=mesh['z'=8,'xl'=2,'c'=2,'y'=8,'xh'=2] {'z','xl'}, dimensions={0} | all-to-all | bytes 1048576 | tf_op jit(solution)/shard_map/all_to_all | solution.py:330
  133.2 0.4 shard_map.108
  133.6 5.8 %shard_map.109 = bf16[128,5120]{1,0:T(8,128)(2,1)} custom-call(bf16[128,1024]{1,0:T(8,128)(2,1)S(1)} %get-tuple-element.24.h_ref, f32[128,128]{1,0:T(8,128)S(1)} %get-tuple-element.25.prob_ref, bf16[8,8,2,64,640]{4,3,2,1,0:T(8,128)(2,1)} %bitcast.30), custom_call_target="tpu_custom_call" | custom-call | flops 1342177280 | bytes 12582912 | tf_op jit(solution)/shard_map/pallas_call | solution.py:280
  (24 shorter events, 0.2 us)
Async XLA Ops:
  7.2 10.1 %copy-start.7 = (bf16[1,160,64]{1,2,0:T(8,128)(2,1)S(1)}, bf16[1,160,64]{1,2,0:T(8,128)(2,1)}, u32[]{:S(2)}) copy-start(bf16[1,160,64]{1,2,0:T(8,128)(2,1)} %param.12) | copy-start | bytes 61444
  7.2 20.3 %copy-start = (bf16[1,1,5120,128]{3,2,1,0:T(8,128)(2,1)S(1)}, bf16[1,1,5120,128]{3,2,1,0:T(8,128)(2,1)}, u32[]{:S(2)}) copy-start(bf16[1,1,5120,128]{3,2,1,0:T(8,128)(2,1)} %param.8) | copy-start | bytes 3932164
  7.2 20.3 %copy-start.5 = (s32[128,1]{0,1:T(1,128)S(1)}, s32[128,1]{0,1:T(1,128)}, u32[]{:S(2)}) copy-start(s32[128,1]{0,1:T(1,128)} %param.14) | copy-start | bytes 1540
  8.4 19.0 %collective-permute-start = (bf16[16,160,128]{2,1,0:T(8,128)(2,1)S(1)}, bf16[16,160,128]{2,1,0:T(8,128)(2,1)S(1)}, u32[]{:S(2)}, u32[]{:S(2)}) collective-permute-start(bf16[16,160,128]{2,1,0:T(8,128)(2,1)S(1)} %dynamic-slice_bitcast_fusion), channel_id=1, source_target_pairs={{0,16},{16,0},{1,17},{17,1},{2,18},{18,2},{3,19},{19,3},{4,20},{20... | collective-permute-start | bytes 1966088 | tf_op jit(solution)/shard_map/ppermute | solution.py:308
  17.9 8.4 %all-to-all-start = ((bf16[4,64,160]{2,1,0:T(8,128)(2,1)}), bf16[4,64,160]{2,1,0:T(8,128)(2,1)S(1)}, u32[]{:S(2)}, u32[]{:S(2)}) async-start(bf16[4,64,160]{2,1,0:T(8,128)(2,1)} %broadcast_in_dim.12), calls=%async_computation | async-start | bytes 262144 | tf_op jit(solution)/shard_map/all_to_all | solution.py:311
  21.2 112.3 %all-gather.3.cloned.1.call-start = ((), (), s32[]{:S(2)}) async-start(), calls=%async_computation.4 | async-start | bytes 10567680 | tf_op jit(solution)/shard_map/all_gather | solution.py:315
  28.5 5.4 %copy-start.1 = (bf16[128,5120]{1,0:T(8,128)(2,1)S(1)}, bf16[128,5120]{1,0:T(8,128)(2,1)}, u32[]{:S(2)}) copy-start(bf16[128,5120]{1,0:T(8,128)(2,1)} %x_ref.1) | copy-start | bytes 3932164
  28.5 24.6 %all-to-all-start.1 = ((bf16[16,176,128]{2,1,0:T(8,128)(2,1)}), bf16[16,176,128]{2,1,0:T(8,128)(2,1)S(1)}, u32[]{:S(2)}, u32[]{:S(2)}) async-start(bf16[16,176,128]{2,1,0:T(8,128)(2,1)} %shard_map.104), calls=%async_computation.1 | async-start | bytes 1441792 | tf_op jit(solution)/shard_map/all_to_all | solution.py:318
  35.6 23.3 %copy-start.2 = (f32[1,160,128]{2,1,0:T(8,128)S(1)}, f32[1,160,128]{2,1,0:T(8,128)}, u32[]{:S(2)}) copy-start(f32[1,160,128]{2,1,0:T(8,128)} %param.9) | copy-start | bytes 245764
  35.6 23.3 %copy-start.3 = (f32[1,160,128]{2,1,0:T(8,128)S(1)}, f32[1,160,128]{2,1,0:T(8,128)}, u32[]{:S(2)}) copy-start(f32[1,160,128]{2,1,0:T(8,128)} %param.10) | copy-start | bytes 245764
  35.6 23.3 %copy-start.4 = (f32[1,160,128]{2,1,0:T(8,128)S(1)}, f32[1,160,128]{2,1,0:T(8,128)}, u32[]{:S(2)}) copy-start(f32[1,160,128]{2,1,0:T(8,128)} %param.11) | copy-start | bytes 245764
  53.0 45.8 %all-to-all-start.2 = ((bf16[16,2,32,640]{3,2,1,0:T(8,128)(2,1)}), bf16[16,2,32,640]{3,2,1,0:T(8,128)(2,1)S(1)}, u32[]{:S(2)}, u32[]{:S(2)}) async-start(bf16[16,2,32,640]{3,2,1,0:T(8,128)(2,1)} %shard_map.103), calls=%async_computation.2 | async-start | bytes 2621440 | tf_op jit(solution)/shard_map/all_to_all | solution.py:320
  59.7 6.2 %collective-permute-start.1 = (bf16[160,128]{1,0:T(8,128)(2,1)S(1)}, bf16[160,128]{1,0:T(8,128)(2,1)S(1)}, u32[]{:S(2)}, u32[]{:S(2)}) collective-permute-start(bf16[160,128]{1,0:T(8,128)(2,1)S(1)} %get-tuple-element.19), channel_id=1, source_target_pairs={{0,1},{1,0},{2,3},{3,2},{4,5},{5,4},{6,7},{7,6},{8,9},{9,8},{10,11... | collective-permute-start | bytes 122888 | tf_op jit(solution)/shard_map/ppermute | solution.py:323
  90.0 11.3 %collective-permute-start.2 = (bf16[16,160,128]{2,1,0:T(8,128)(2,1)S(1)}, bf16[16,160,128]{2,1,0:T(8,128)(2,1)S(1)}, u32[]{:S(2)}, u32[]{:S(2)}) collective-permute-start(bf16[16,160,128]{2,1,0:T(8,128)(2,1)S(1)} %bitcast.21), channel_id=1, source_target_pairs={{0,16},{16,0},{1,17},{17,1},{2,18},{18,2},{3,19},{19,3},{4,20},{20... | collective-permute-start | bytes 1966088 | tf_op jit(solution)/shard_map/ppermute | solution.py:325
  101.3 31.8 %copy-start.6 = (f32[128]{0:T(128)S(1)}, f32[128]{0:T(128)}, u32[]{:S(2)}) copy-start(f32[128]{0:T(128)} %param.15) | copy-start | bytes 1540
Sparse Core Ops, SparseCore 0:
  27.6 104.2 all-gather.2
